TPU v7x, 128 devices: a whole 4x4x4 slice. The times are simulated.
128 devices in a mesh: ctx: 16 (over x, y_lo, core), expert: 8 (over z, y_hi).
Axes of the slice: x: 4, y: 4 (y_hi: 2, y_lo: 2; y = y_hi * 2 + y_lo), z: 4, core: 2. Of those that a mesh axis runs over, the one named last changes fastest.
Arguments:
- block_input: bfloat16 [8, 2048, 768], P('expert', 'ctx'), may hold values from -6 to 6
- gain_one: float32 [768], replicated, may hold values from 0.5 to 1.5
- qkv_weight: bfloat16 [3, 768, 768], replicated, may hold values from -0.21875 to 0.21875
- out_weight: bfloat16 [768, 768], replicated, may hold values from -0.5 to 0.5
- rel_table: float32 [32, 12], replicated, may hold values from -4 to 4
- gain_two: float32 [768], replicated, may hold values from 0.5 to 1.5
- router_weight: bfloat16 [768, 8], replicated, may hold values from -0.15625 to 0.15625
- routes: int32 [8, 2048, 1], P('expert', 'ctx'), may hold values from 0 to 7; in each aligned block of 128 rows (0 to 127, 128 to 255, ..., all dimensions but the last counted through in order) at most 24 rows name the same one
- w_in: bfloat16 [8, 768, 3072], P('expert'), may hold values from -0.21875 to 0.21875
- w_out: bfloat16 [8, 3072, 768], P('expert'), may hold values from -0.875 to 0.875
- cotangent: bfloat16 [8, 2048, 768], P('expert', 'ctx'), may hold values from -6 to 6
Outputs:
- block_output: bfloat16 [8, 2048, 768], P('expert', 'ctx')
- grad_input: float32 [8, 2048, 768], P('expert', 'ctx')
- grad_gain_one: float32 [768], P(('ctx', 'expert'))
- grad_qkv: float32 [3, 768, 768], P(None, ('ctx', 'expert'))
- grad_out: float32 [768, 768], P(('ctx', 'expert'))
- grad_table: float32 [32, 12], replicated
- grad_gain_two: float32 [768], P(('ctx', 'expert'))
- grad_router: float32 [768, 8], P(('ctx', 'expert'))
- grad_w_in: float32 [8, 768, 3072], P('expert', 'ctx')
- grad_w_out: float32 [8, 3072, 768], P('expert', 'ctx')
Inputs may be any that keep to these rules, and one draw needn't show every extreme that they name: `routes`: each token names one expert; taking all sequences' tokens in order in aligned blocks of 128 (the rows of one device), no expert is named more than 24 times in a block, a bound that some block reaches.
All inputs are finite; a program needn't handle non-finite values.
Results may differ from a plain program's by a relative error of at most 0.04.
Values may be sent and summed in bfloat16 or wider, within the bound.
A program may use at most 128 MiB of HBM per device.

v0:
```python
import jax
import jax.numpy as jnp
import numpy as np
from jax import lax
from jax.sharding import PartitionSpec as P

HEADS = 12
HEAD_DIM = 64
BUCKETS = 32
MAX_DISTANCE = 128


EPSILON = 1e-06
HIGH = lax.Precision.HIGHEST


def shortened(shard):
    return jax.tree.map(lambda a: a.astype(jnp.bfloat16) if a.dtype == jnp.float32 else a, shard)


def from_behind(value, axis, steps):
    count = lax.axis_size(axis)
    pairs = [(source, (source + steps) % count) for source in range(count)]
    return lax.ppermute(value, axis, pairs)


def bucket_edges(buckets, reach):
    half = buckets // 2
    exact = half // 2
    spans = np.arange(1, reach + 1)
    spread = np.log(np.maximum(spans, exact) / exact) / np.log(reach / exact) * (half - exact)
    large = np.minimum(exact + spread.astype(np.int64), half - 1)
    level = np.where(spans < exact, spans, large)
    return [int(np.argmax(level >= b)) + 1 for b in range(1, half)]


def bucket_of(offset):
    half = BUCKETS // 2
    length = jnp.abs(offset)
    level = jnp.where(offset > 0, half, 0).astype(jnp.int32)
    for edge in bucket_edges(BUCKETS, MAX_DISTANCE):
        level = level + (length >= edge).astype(jnp.int32)
    return level


def rms_norm(rows, gain):
    return rows * lax.rsqrt(jnp.mean(rows * rows, axis=-1, keepdims=True) + EPSILON) * gain


def offsets_near(query_first, query_count, key_first, key_count):
    offset = (key_first + jnp.arange(key_count, dtype=jnp.int32))[None, :] - (
        query_first + jnp.arange(query_count, dtype=jnp.int32)
    )[:, None]
    near = jnp.logical_and(
        key_first < query_first + query_count + MAX_DISTANCE,
        key_first + key_count > query_first - MAX_DISTANCE,
    )
    return (offset, near)


def bias_block(table, query_first, query_count, key_first, key_count):
    offset, near = offsets_near(query_first, query_count, key_first, key_count)

    def close(values):
        indicator = (bucket_of(offset)[:, :, None] == jnp.arange(BUCKETS, dtype=jnp.int32)).astype(
            jnp.float32
        )
        return jnp.einsum("qkb,bh->hqk", indicator, values, precision=HIGH)

    def distant(values):
        return jnp.where(
            offset[None] > 0,
            values[BUCKETS - 1][:, None, None],
            values[BUCKETS // 2 - 1][:, None, None],
        )

    return lax.cond(near, close, distant, table)


def bias_grad(grad_scores, query_first, query_count, key_first, key_count):
    offset, near = offsets_near(query_first, query_count, key_first, key_count)

    def close(grads):
        indicator = (bucket_of(offset)[:, :, None] == jnp.arange(BUCKETS, dtype=jnp.int32)).astype(
            jnp.float32
        )
        return jnp.einsum("qkb,hqk->bh", indicator, grads, precision=HIGH)

    def distant(grads):
        after = jnp.sum(jnp.where(offset[None] > 0, grads, 0.0), axis=(1, 2))
        before = jnp.sum(jnp.where(offset[None] < 0, grads, 0.0), axis=(1, 2))
        level = jnp.arange(BUCKETS, dtype=jnp.int32)[:, None]
        return jnp.where(level == BUCKETS - 1, after[None, :], 0.0) + jnp.where(
            level == BUCKETS // 2 - 1, before[None, :], 0.0
        )

    return lax.cond(near, close, distant, grad_scores)


def fold_keys(carry, piece, query_heads, query_first, table, span_rows):
    keys, values = piece
    count = keys.shape[0]
    query_count = query_heads.shape[0]

    def one_span(index, state):
        top, total, weighted = state
        begin = index * span_rows
        key_part = lax.dynamic_slice_in_dim(keys, begin, span_rows, 0).reshape(
            span_rows, HEADS, HEAD_DIM
        )
        value_part = lax.dynamic_slice_in_dim(values, begin, span_rows, 0).reshape(
            span_rows, HEADS, HEAD_DIM
        )
        raw = jnp.einsum("qhd,khd->hqk", query_heads, key_part, preferred_element_type=jnp.float32)
        scores = raw * HEAD_DIM ** (-0.5) + bias_block(
            table, query_first, query_count, begin, span_rows
        )
        new_top = jnp.maximum(top, jnp.max(scores, axis=2))
        weights = jnp.exp(scores - new_top[:, :, None])
        fade = jnp.exp(top - new_top)
        total = total * fade + jnp.sum(weights, axis=2)
        weighted = weighted * fade.T[:, :, None] + jnp.einsum(
            "hqk,khd->qhd",
            weights.astype(jnp.bfloat16),
            value_part,
            preferred_element_type=jnp.float32,
        )
        return (new_top, total, weighted)

    return lax.fori_loop(0, count // span_rows, one_span, carry)


def block_grads(
    query_heads,
    grad_heads,
    log_total,
    row_sums,
    query_first,
    key_heads,
    value_heads,
    key_first,
    table,
):
    query_count = query_heads.shape[0]
    key_count = key_heads.shape[0]
    raw = jnp.einsum("qhd,khd->hqk", query_heads, key_heads, preferred_element_type=jnp.float32)
    scores = raw * HEAD_DIM ** (-0.5) + bias_block(
        table, query_first, query_count, key_first, key_count
    )
    probs = jnp.exp(scores - log_total[:, :, None])
    grad_probs = jnp.einsum(
        "qhd,khd->hqk", grad_heads, value_heads, preferred_element_type=jnp.float32
    )
    grad_scores = probs * (grad_probs - row_sums[:, :, None])
    grad_bias = bias_grad(grad_scores, query_first, query_count, key_first, key_count)
    grad_raw = (grad_scores * HEAD_DIM ** (-0.5)).astype(jnp.bfloat16)
    grad_query = jnp.einsum(
        "hqk,khd->qhd", grad_raw, key_heads, preferred_element_type=jnp.float32
    ).reshape(query_count, -1)
    grad_key = jnp.einsum(
        "hqk,qhd->khd", grad_raw, query_heads, preferred_element_type=jnp.float32
    ).reshape(key_count, -1)
    grad_value = jnp.einsum(
        "hqk,qhd->khd", probs.astype(jnp.bfloat16), grad_heads, preferred_element_type=jnp.float32
    ).reshape(key_count, -1)
    return (grad_query, grad_key, grad_value, grad_bias)


def around_cycle(moving, riders, local, step_fn):
    rounds = lax.axis_size("ctx")
    place = lax.axis_index("ctx")

    def turn(step, carry):
        moving, riders, local = carry
        owner = (place - step + rounds) % rounds
        riders, local = step_fn(moving, riders, owner, local)
        riders = jax.tree.map(
            lambda part, own: part.astype(own.dtype),
            from_behind(shortened(riders), "ctx", 1),
            riders,
        )
        moving = from_behind((moving[0], moving[1]), "ctx", 1)
        return (moving, riders, local)

    moving, riders, local = lax.fori_loop(0, rounds, turn, (moving, riders, local))
    return (riders, local)


def body(
    block_input,
    gain_one,
    qkv_weight,
    out_weight,
    rel_table,
    gain_two,
    router_weight,
    routes,
    w_in,
    w_out,
    cotangent,
):
    count = block_input.shape[1]
    width = block_input.shape[2]
    query_first = lax.axis_index("ctx") * count
    inputs = block_input[0].astype(jnp.float32)
    normed_low = rms_norm(inputs, gain_one).astype(jnp.bfloat16)
    projected = jnp.einsum(
        "td,pde->pte", normed_low, qkv_weight, preferred_element_type=jnp.float32
    ).astype(jnp.bfloat16)
    queries, keys, values = (projected[0], projected[1], projected[2])
    query_heads = queries.reshape(count, HEADS, HEAD_DIM)
    initial = (
        jnp.full((HEADS, count), -1e30, jnp.float32),
        jnp.zeros((HEADS, count), jnp.float32),
        jnp.zeros((count, HEADS, HEAD_DIM), jnp.float32),
    )
    top, total, weighted = fold_keys(
        initial,
        (
            lax.all_gather(keys, "ctx", axis=0, tiled=True),
            lax.all_gather(values, "ctx", axis=0, tiled=True),
        ),
        query_heads,
        query_first,
        rel_table,
        4 * count,
    )
    log_total = top + jnp.log(total)
    core = weighted / total.T[:, :, None]
    attended = core.reshape(count, width).astype(jnp.bfloat16)
    middle = inputs + jnp.dot(attended, out_weight, preferred_element_type=jnp.float32)
    normed_two = rms_norm(middle, gain_two).astype(jnp.bfloat16)
    experts = router_weight.shape[1]
    capacity = 3 * count // (2 * experts)
    choose = routes[0] == jnp.arange(experts, dtype=jnp.int32)[None, :]

    def route_gate(rows_two, router_rows):
        logits = jnp.dot(rows_two, router_rows, precision=HIGH)
        shifted = jnp.exp(logits - jnp.max(logits, axis=1, keepdims=True))
        router = shifted / jnp.sum(shifted, axis=1, keepdims=True)
        return jnp.sum(jnp.where(choose, router, 0.0), axis=1)

    gate, gate_back = jax.vjp(
        route_gate, normed_two.astype(jnp.float32), router_weight.astype(jnp.float32)
    )
    ranks = jnp.cumsum(choose.astype(jnp.int32), axis=0) - 1
    slot = jnp.sum(jnp.where(choose, ranks, 0), axis=1)
    target = routes[0][:, 0] * capacity + slot
    select = (jnp.arange(experts * capacity, dtype=jnp.int32)[:, None] == target[None, :]).astype(
        jnp.bfloat16
    )
    outgoing = jnp.dot(select, normed_two, preferred_element_type=jnp.float32).astype(jnp.bfloat16)
    arrived = lax.all_to_all(
        outgoing.reshape(experts, capacity, width),
        "expert",
        split_axis=0,
        concat_axis=0,
        tiled=True,
    ).reshape(experts * capacity, width)
    inner = jnp.dot(arrived, w_in[0], preferred_element_type=jnp.float32)
    hidden = jax.nn.gelu(inner, approximate=True).astype(jnp.bfloat16)
    produced = jnp.dot(hidden, w_out[0], preferred_element_type=jnp.float32).astype(jnp.bfloat16)
    returned = lax.all_to_all(
        produced.reshape(experts, capacity, width),
        "expert",
        split_axis=0,
        concat_axis=0,
        tiled=True,
    ).reshape(experts * capacity, width)
    back_rows = jnp.einsum("rt,rd->td", select, returned, preferred_element_type=jnp.float32)
    output = middle + gate[:, None] * back_rows
    grad_output = cotangent[0].astype(jnp.float32)
    grad_returned = (gate[:, None] * grad_output).astype(jnp.bfloat16)
    grad_gate = jnp.sum(grad_output * back_rows, axis=1)
    going = jnp.dot(select, grad_returned, preferred_element_type=jnp.float32).astype(jnp.bfloat16)
    grad_produced = lax.all_to_all(
        going.reshape(experts, capacity, width), "expert", split_axis=0, concat_axis=0, tiled=True
    ).reshape(experts * capacity, width)
    grad_w_out_local = jnp.einsum(
        "rf,rd->fd", hidden, grad_produced, preferred_element_type=jnp.float32
    )
    grad_hidden = jnp.einsum(
        "rd,fd->rf", grad_produced, w_out[0], preferred_element_type=jnp.float32
    )
    gelu_back = jax.vjp(lambda value: jax.nn.gelu(value, approximate=True), inner)[1]
    grad_inner = gelu_back(grad_hidden)[0].astype(jnp.bfloat16)
    grad_w_in_local = jnp.einsum(
        "rd,rf->df", arrived, grad_inner, preferred_element_type=jnp.float32
    )
    grad_arrived = jnp.einsum(
        "rf,df->rd", grad_inner, w_in[0], preferred_element_type=jnp.float32
    ).astype(jnp.bfloat16)
    grad_outgoing = lax.all_to_all(
        grad_arrived.reshape(experts, capacity, width),
        "expert",
        split_axis=0,
        concat_axis=0,
        tiled=True,
    ).reshape(experts * capacity, width)
    grad_normed_two = jnp.einsum(
        "rt,rd->td", select, grad_outgoing, preferred_element_type=jnp.float32
    )
    grad_two_router, grad_router_local = gate_back(grad_gate)
    grad_normed_two = grad_normed_two + grad_two_router
    norm_back_two = jax.vjp(rms_norm, middle, gain_two)[1]
    grad_middle_part, grad_gain_two_local = norm_back_two(grad_normed_two)
    grad_middle = grad_output + grad_middle_part
    grad_mixed = grad_middle.astype(jnp.bfloat16)
    grad_out_local = jnp.einsum(
        "td,te->de", attended, grad_mixed, preferred_element_type=jnp.float32
    )
    grad_attended = jnp.einsum(
        "te,de->td", grad_mixed, out_weight, preferred_element_type=jnp.float32
    ).astype(jnp.bfloat16)
    grad_heads = grad_attended.reshape(count, HEADS, HEAD_DIM)
    row_sums = jnp.einsum("qhd,qhd->hq", grad_heads.astype(jnp.float32), core, precision=HIGH)
    zero_rows = jnp.zeros((count, width), jnp.float32)
    zero_table = jnp.zeros((BUCKETS, HEADS), jnp.float32)

    def step_keys(moving, riders, owner, local):
        key_rows, value_rows = moving
        grad_query, grad_key, grad_value, grad_bias = block_grads(
            query_heads,
            grad_heads,
            log_total,
            row_sums,
            query_first,
            key_rows.reshape(count, HEADS, HEAD_DIM),
            value_rows.reshape(count, HEADS, HEAD_DIM),
            owner * count,
            rel_table,
        )
        return (
            (riders[0] + grad_key, riders[1] + grad_value),
            (local[0] + grad_query, local[1] + grad_bias),
        )

    riders, local = around_cycle(
        (keys, values), (zero_rows, zero_rows), (zero_rows, zero_table), step_keys
    )
    grad_keys, grad_values = riders
    grad_queries, table_local = local
    grad_projected = jnp.stack([grad_queries, grad_keys, grad_values]).astype(jnp.bfloat16)
    grad_qkv_local = jnp.einsum(
        "td,pte->pde", normed_low, grad_projected, preferred_element_type=jnp.float32
    )
    grad_normed = jnp.einsum(
        "pte,pde->td", grad_projected, qkv_weight, preferred_element_type=jnp.float32
    )
    norm_back_one = jax.vjp(rms_norm, inputs, gain_one)[1]
    grad_input_part, grad_gain_one_local = norm_back_one(grad_normed)
    grad_input = grad_middle + grad_input_part
    grad_gain_one, grad_qkv, grad_out, grad_gain_two, grad_router = (
        lax.psum_scatter(grad_gain_one_local, ("ctx", "expert"), scatter_dimension=0, tiled=True),
        lax.psum_scatter(grad_qkv_local, ("ctx", "expert"), scatter_dimension=1, tiled=True),
        lax.psum_scatter(grad_out_local, ("ctx", "expert"), scatter_dimension=0, tiled=True),
        lax.psum_scatter(grad_gain_two_local, ("ctx", "expert"), scatter_dimension=0, tiled=True),
        lax.psum_scatter(grad_router_local, ("ctx", "expert"), scatter_dimension=0, tiled=True),
    )
    grad_table = lax.psum(table_local, ("ctx", "expert"))
    grad_w_in, grad_w_out = (
        lax.psum_scatter(
            grad_w_in_local[None].astype(jnp.bfloat16), "ctx", scatter_dimension=1, tiled=True
        ).astype(jnp.float32),
        lax.psum_scatter(
            grad_w_out_local[None].astype(jnp.bfloat16), "ctx", scatter_dimension=1, tiled=True
        ).astype(jnp.float32),
    )
    return (
        output.astype(jnp.bfloat16).reshape(1, count, width),
        grad_input.reshape(1, count, width),
        grad_gain_one,
        grad_qkv,
        grad_out,
        grad_table,
        grad_gain_two,
        grad_router,
        grad_w_in,
        grad_w_out,
    )


def solution(mesh):
    placed = (
        P("expert", "ctx", None),
        P(),
        P(),
        P(),
        P(),
        P(),
        P(),
        P("expert", "ctx", None),
        P("expert", None, None),
        P("expert", None, None),
        P("expert", "ctx", None),
    )
    return jax.shard_map(
        body,
        mesh=mesh,
        in_specs=placed,
        out_specs=(
            P("expert", "ctx", None),
            P("expert", "ctx", None),
            P(("ctx", "expert")),
            P(None, ("ctx", "expert"), None),
            P(("ctx", "expert"), None),
            P(),
            P(("ctx", "expert")),
            P(("ctx", "expert"), None),
            P("expert", "ctx", None),
            P("expert", "ctx", None),
        ),
        check_vma=False,
    )
```

profile of v0, /device:TPU:1, one launch (start us, length us, event | category | flops | bytes accessed | tf_op | source)
XLA Modules:
  0.0 1678.6 jit_solution(10310760539735719595)
XLA Ops:
  22.1 29.2 %all-gather.7.cloned.1.call-done = bf16[1,2048,768]{2,1,0:T(8,128)(2,1)} async-done(((bf16[1,128,768]{2,1,0:T(8,128)(2,1)}), bf16[1,2048,768]{2,1,0:T(8,128)(2,1)}) %all-gather.7.cloned.1.call-update) | async-done | bytes 3145744 | tf_op jit(solution)/shard_map/all_gather | solution.py:221
  51.3 37.7 %all-gather.5.cloned.1.call-done = bf16[1,2048,768]{2,1,0:T(8,128)(2,1)} async-done(((bf16[1,128,768]{2,1,0:T(8,128)(2,1)}), bf16[1,2048,768]{2,1,0:T(8,128)(2,1)}) %all-gather.5.cloned.1.call-update) | async-done | bytes 3145744 | tf_op jit(solution)/shard_map/all_gather | solution.py:220
  89.0 93.6 %while.46 = (s32[]{:T(128)}, f32[12,128]{1,0:T(8,128)S(1)}, f32[12,128]{1,0:T(8,128)}, f32[128,12,64]{0,2,1:T(8,128)}, bf16[2048,768]{1,0:T(8,128)(2,1)}, /*inde...) while((s32[]{:T(128)}, f32[12,128]{1,0:T(8,128)S(1)}, ...), condition=%wide.region_6.7_spmd.clone, body=%wide.region_1.6_spmd.clone.sunk | while | flops 514434688 | bytes 38362016 | solution.py:130
  97.1 5.6 conditional.9
  188.0 6.5 all-to-all-start
  196.7 6.6 all-to-all-done
  206.8 5.4 fusion.60
  218.1 6.1 all-to-all-done.1
  243.8 5.6 fusion.53
  260.7 5.8 all-to-all-done.3
  278.3 773.7 %while.47 = (s32[]{:T(128)}, bf16[128,768]{0,1:T(8,128)(2,1)}, bf16[128,768]{0,1:T(8,128)(2,1)}, f32[128,768]{0,1:T(8,128)}, f32[128,768]{0,1:T(8,128)}, /*index...) while((s32[]{:T(128)}, bf16[128,768]{0,1:T(8,128)(2,1)}, ...), condition=%wide.region_25.26_spmd.clone, body=%wide.region_18.25_spmd.clone.sunk | while | flops 282412032 | bytes 32684328 | solution.py:185
  279.9 5.4 collective-permute-start
  301.6 8.9 collective-permute-start.3
  312.5 6.5 conditional.11
  339.4 8.5 collective-permute-start.2
  348.8 8.9 collective-permute-start.3
  359.8 6.5 conditional.11
  389.3 8.5 collective-permute-start.2
  398.8 8.9 collective-permute-start.3
  427.1 5.4 conditional.10
  437.8 8.5 collective-permute-start.2
  447.3 8.9 collective-permute-start.3
  475.6 5.4 conditional.10
  486.3 8.5 collective-permute-start.2
  495.7 8.9 collective-permute-start.3
  524.1 5.4 conditional.10
  534.8 8.5 collective-permute-start.2
  544.2 8.9 collective-permute-start.3
  572.6 5.4 conditional.10
  583.3 8.5 collective-permute-start.2
  592.7 8.9 collective-permute-start.3
  621.1 5.4 conditional.10
  631.8 8.5 collective-permute-start.2
  641.2 8.9 collective-permute-start.3
  669.6 5.4 conditional.10
  680.3 8.5 collective-permute-start.2
  689.7 8.9 collective-permute-start.3
  718.1 5.4 conditional.10
  728.8 8.5 collective-permute-start.2
  738.2 8.9 collective-permute-start.3
  766.6 5.4 conditional.10
  777.3 8.5 collective-permute-start.2
  786.7 8.9 collective-permute-start.3
  815.1 5.4 conditional.10
  825.8 8.5 collective-permute-start.2
  835.2 8.9 collective-permute-start.3
  863.6 5.4 conditional.10
  874.3 8.5 collective-permute-start.2
  883.7 8.9 collective-permute-start.3
  922.8 8.5 collective-permute-start.2
  932.2 8.9 collective-permute-start.3
  971.3 8.5 collective-permute-start.2
  980.7 8.9 collective-permute-start.3
  1017.9 9.1 collective-permute-start.2
  1028.0 8.9 collective-permute-start.3
  1038.9 6.5 conditional.11
  1062.7 11.1 copy.110
  1073.8 5.8 fusion.46
  1088.3 349.5 %fusion = f32[8,768]{1,0:T(8,128)} fusion(f32[768,768]{1,0:T(8,128)} %fusion.80), kind=kCustom, calls=%all-reduce-scatter | all-reduce-scatter fusion | flops 786433 | bytes 2383872
  1446.3 17.1 %collective-permute-start.31 = (f32[8,768]{1,0:T(8,128)}, f32[8,768]{1,0:T(8,128)}, u32[]{:S(2)}, u32[]{:S(2)}) collective-permute-start(f32[8,768]{1,0:T(8,128)} %fusion), channel_id=1, source_target_pairs={{0,28},{1,29},{2,30},{3,31},{4,32},{5,33},{6,34},{7,35},{8,36},{9,... | collective-permute-start | bytes 73736
  1479.0 6.6 collective-permute-start.23
  1496.1 5.4 collective-permute-start.18
  1526.5 66.9 %all-reduce.6 = (f32[768]{0:T(1024)}, f32[32,12]{0,1:T(8,128)}, f32[768]{0:T(1024)S(1)}, f32[768,8]{1,0:T(8,128)}) all-reduce(f32[768]{0:T(1024)} %get-tuple-element.934, f32[32,12]{0,1:T(8,128)S(1)} %copy-done.24, f32[768]{0:T(1024)S(1)} %copy-done.41, f32[768,8]{1,0:T(8,128)} %fusion.96), channel_id=4, replica_groups=mesh['ctx'=16,'expert'=8] {'ctx','expert'}, use_global_device_ids=true, to_apply=%region_28.29.clone | all-reduce | flops 8064 | bytes 64512
  1618.4 47.1 %concatenate = f32[262,768]{1,0:T(8,128)} concatenate(f32[6,768]{1,0:T(8,128)} %copy-done.28, f32[8,768]{1,0:T(8,128)} %collective-permute-done.34, f32[8,768]{1,0:T(8,128)} %collective-permute-done.33, f32[8,768]{1,0:T(8,128)} %collective-permute-done.32, f32[8,768]{1,0:T(8,128)} %collective-permute-done.31, f32[8,768]{1,0:T(8,128)} %collective-permute-done.30, ...), dimensions={0} | concatenate | bytes 1609728
  (1093 shorter events, 882.1 us)
Async XLA Ops:
  7.2 44.1 %all-gather.7.cloned.1.call-start = ((), (), s32[]{:S(2)}) async-start(), calls=%async_computation.9 | async-start | bytes 3342336 | tf_op jit(solution)/shard_map/all_gather | solution.py:221
  11.9 77.1 %all-gather.5.cloned.1.call-start = ((), (), s32[]{:S(2)}) async-start(), calls=%async_computation.8 | async-start | bytes 3342336 | tf_op jit(solution)/shard_map/all_gather | solution.py:220
  258.7 1408.2 %all-reduce.9.cloned.1.call-start = ((), (), s32[]{:S(2)}) async-start(), calls=%async_computation.10 | async-start | bytes 18874368
  279.9 45.0 %collective-permute-start = (bf16[128,768]{0,1:T(8,128)(2,1)}, bf16[128,768]{0,1:T(8,128)(2,1)}, u32[]{:S(2)}, u32[]{:S(2)}) collective-permute-start(bf16[128,768]{0,1:T(8,128)(2,1)} %copy.159), channel_id=1, source_target_pairs={{0,8},{8,16},{16,24},{24,32},{32,40},{40,48},{48,56},{56,64},{64,7... | collective-permute-start | bytes 589832 | tf_op jit(solution)/shard_map/while/body/eval_jaxpr/ppermute | solution.py:24
  287.0 37.9 %collective-permute-start.1 = (bf16[128,768]{0,1:T(8,128)(2,1)}, bf16[128,768]{0,1:T(8,128)(2,1)}, u32[]{:S(2)}, u32[]{:S(2)}) collective-permute-start(bf16[128,768]{0,1:T(8,128)(2,1)} %copy.160), channel_id=1, source_target_pairs={{0,8},{8,16},{16,24},{24,32},{32,40},{40,48},{48,56},{56,64},{64,7... | collective-permute-start | bytes 589832 | tf_op jit(solution)/shard_map/while/body/eval_jaxpr/ppermute | solution.py:24
  296.5 25.0 %collective-permute-start.2 = (bf16[128,768]{0,1:T(8,128)(2,1)}, bf16[128,768]{0,1:T(8,128)(2,1)}, u32[]{:S(2)}, u32[]{:S(2)}) collective-permute-start(bf16[128,768]{0,1:T(8,128)(2,1)} %fusion.187), channel_id=1, source_target_pairs={{0,8},{8,16},{16,24},{24,32},{32,40},{40,48},{48,56},{56,64},{64,7... | collective-permute-start | bytes 589832 | tf_op jit(solution)/shard_map/while/body/eval_jaxpr/ppermute | solution.py:24
  326.5 46.4 %collective-permute-start = (bf16[128,768]{0,1:T(8,128)(2,1)}, bf16[128,768]{0,1:T(8,128)(2,1)}, u32[]{:S(2)}, u32[]{:S(2)}) collective-permute-start(bf16[128,768]{0,1:T(8,128)(2,1)} %copy.159), channel_id=1, source_target_pairs={{0,8},{8,16},{16,24},{24,32},{32,40},{40,48},{48,56},{56,64},{64,7... | collective-permute-start | bytes 589832 | tf_op jit(solution)/shard_map/while/body/eval_jaxpr/ppermute | solution.py:24
  329.7 43.2 %collective-permute-start.1 = (bf16[128,768]{0,1:T(8,128)(2,1)}, bf16[128,768]{0,1:T(8,128)(2,1)}, u32[]{:S(2)}, u32[]{:S(2)}) collective-permute-start(bf16[128,768]{0,1:T(8,128)(2,1)} %copy.160), channel_id=1, source_target_pairs={{0,8},{8,16},{16,24},{24,32},{32,40},{40,48},{48,56},{56,64},{64,7... | collective-permute-start | bytes 589832 | tf_op jit(solution)/shard_map/while/body/eval_jaxpr/ppermute | solution.py:24
  339.4 30.1 %collective-permute-start.2 = (bf16[128,768]{0,1:T(8,128)(2,1)}, bf16[128,768]{0,1:T(8,128)(2,1)}, u32[]{:S(2)}, u32[]{:S(2)}) collective-permute-start(bf16[128,768]{0,1:T(8,128)(2,1)} %fusion.187), channel_id=1, source_target_pairs={{0,8},{8,16},{16,24},{24,32},{32,40},{40,48},{48,56},{56,64},{64,7... | collective-permute-start | bytes 589832 | tf_op jit(solution)/shard_map/while/body/eval_jaxpr/ppermute | solution.py:24
  374.5 46.9 %collective-permute-start = (bf16[128,768]{0,1:T(8,128)(2,1)}, bf16[128,768]{0,1:T(8,128)(2,1)}, u32[]{:S(2)}, u32[]{:S(2)}) collective-permute-start(bf16[128,768]{0,1:T(8,128)(2,1)} %copy.159), channel_id=1, source_target_pairs={{0,8},{8,16},{16,24},{24,32},{32,40},{40,48},{48,56},{56,64},{64,7... | collective-permute-start | bytes 589832 | tf_op jit(solution)/shard_map/while/body/eval_jaxpr/ppermute | solution.py:24
  377.8 43.6 %collective-permute-start.1 = (bf16[128,768]{0,1:T(8,128)(2,1)}, bf16[128,768]{0,1:T(8,128)(2,1)}, u32[]{:S(2)}, u32[]{:S(2)}) collective-permute-start(bf16[128,768]{0,1:T(8,128)(2,1)} %copy.160), channel_id=1, source_target_pairs={{0,8},{8,16},{16,24},{24,32},{32,40},{40,48},{48,56},{56,64},{64,7... | collective-permute-start | bytes 589832 | tf_op jit(solution)/shard_map/while/body/eval_jaxpr/ppermute | solution.py:24
  389.3 28.7 %collective-permute-start.2 = (bf16[128,768]{0,1:T(8,128)(2,1)}, bf16[128,768]{0,1:T(8,128)(2,1)}, u32[]{:S(2)}, u32[]{:S(2)}) collective-permute-start(bf16[128,768]{0,1:T(8,128)(2,1)} %fusion.187), channel_id=1, source_target_pairs={{0,8},{8,16},{16,24},{24,32},{32,40},{40,48},{48,56},{56,64},{64,7... | collective-permute-start | bytes 589832 | tf_op jit(solution)/shard_map/while/body/eval_jaxpr/ppermute | solution.py:24
  423.0 46.9 %collective-permute-start = (bf16[128,768]{0,1:T(8,128)(2,1)}, bf16[128,768]{0,1:T(8,128)(2,1)}, u32[]{:S(2)}, u32[]{:S(2)}) collective-permute-start(bf16[128,768]{0,1:T(8,128)(2,1)} %copy.159), channel_id=1, source_target_pairs={{0,8},{8,16},{16,24},{24,32},{32,40},{40,48},{48,56},{56,64},{64,7... | collective-permute-start | bytes 589832 | tf_op jit(solution)/shard_map/while/body/eval_jaxpr/ppermute | solution.py:24
  426.3 43.6 %collective-permute-start.1 = (bf16[128,768]{0,1:T(8,128)(2,1)}, bf16[128,768]{0,1:T(8,128)(2,1)}, u32[]{:S(2)}, u32[]{:S(2)}) collective-permute-start(bf16[128,768]{0,1:T(8,128)(2,1)} %copy.160), channel_id=1, source_target_pairs={{0,8},{8,16},{16,24},{24,32},{32,40},{40,48},{48,56},{56,64},{64,7... | collective-permute-start | bytes 589832 | tf_op jit(solution)/shard_map/while/body/eval_jaxpr/ppermute | solution.py:24
  437.8 28.7 %collective-permute-start.2 = (bf16[128,768]{0,1:T(8,128)(2,1)}, bf16[128,768]{0,1:T(8,128)(2,1)}, u32[]{:S(2)}, u32[]{:S(2)}) collective-permute-start(bf16[128,768]{0,1:T(8,128)(2,1)} %fusion.187), channel_id=1, source_target_pairs={{0,8},{8,16},{16,24},{24,32},{32,40},{40,48},{48,56},{56,64},{64,7... | collective-permute-start | bytes 589832 | tf_op jit(solution)/shard_map/while/body/eval_jaxpr/ppermute | solution.py:24
  471.5 46.9 %collective-permute-start = (bf16[128,768]{0,1:T(8,128)(2,1)}, bf16[128,768]{0,1:T(8,128)(2,1)}, u32[]{:S(2)}, u32[]{:S(2)}) collective-permute-start(bf16[128,768]{0,1:T(8,128)(2,1)} %copy.159), channel_id=1, source_target_pairs={{0,8},{8,16},{16,24},{24,32},{32,40},{40,48},{48,56},{56,64},{64,7... | collective-permute-start | bytes 589832 | tf_op jit(solution)/shard_map/while/body/eval_jaxpr/ppermute | solution.py:24
  474.8 43.6 %collective-permute-start.1 = (bf16[128,768]{0,1:T(8,128)(2,1)}, bf16[128,768]{0,1:T(8,128)(2,1)}, u32[]{:S(2)}, u32[]{:S(2)}) collective-permute-start(bf16[128,768]{0,1:T(8,128)(2,1)} %copy.160), channel_id=1, source_target_pairs={{0,8},{8,16},{16,24},{24,32},{32,40},{40,48},{48,56},{56,64},{64,7... | collective-permute-start | bytes 589832 | tf_op jit(solution)/shard_map/while/body/eval_jaxpr/ppermute | solution.py:24
  486.3 28.7 %collective-permute-start.2 = (bf16[128,768]{0,1:T(8,128)(2,1)}, bf16[128,768]{0,1:T(8,128)(2,1)}, u32[]{:S(2)}, u32[]{:S(2)}) collective-permute-start(bf16[128,768]{0,1:T(8,128)(2,1)} %fusion.187), channel_id=1, source_target_pairs={{0,8},{8,16},{16,24},{24,32},{32,40},{40,48},{48,56},{56,64},{64,7... | collective-permute-start | bytes 589832 | tf_op jit(solution)/shard_map/while/body/eval_jaxpr/ppermute | solution.py:24
  520.0 46.9 %collective-permute-start = (bf16[128,768]{0,1:T(8,128)(2,1)}, bf16[128,768]{0,1:T(8,128)(2,1)}, u32[]{:S(2)}, u32[]{:S(2)}) collective-permute-start(bf16[128,768]{0,1:T(8,128)(2,1)} %copy.159), channel_id=1, source_target_pairs={{0,8},{8,16},{16,24},{24,32},{32,40},{40,48},{48,56},{56,64},{64,7... | collective-permute-start | bytes 589832 | tf_op jit(solution)/shard_map/while/body/eval_jaxpr/ppermute | solution.py:24
  523.3 43.6 %collective-permute-start.1 = (bf16[128,768]{0,1:T(8,128)(2,1)}, bf16[128,768]{0,1:T(8,128)(2,1)}, u32[]{:S(2)}, u32[]{:S(2)}) collective-permute-start(bf16[128,768]{0,1:T(8,128)(2,1)} %copy.160), channel_id=1, source_target_pairs={{0,8},{8,16},{16,24},{24,32},{32,40},{40,48},{48,56},{56,64},{64,7... | collective-permute-start | bytes 589832 | tf_op jit(solution)/shard_map/while/body/eval_jaxpr/ppermute | solution.py:24
  534.8 28.7 %collective-permute-start.2 = (bf16[128,768]{0,1:T(8,128)(2,1)}, bf16[128,768]{0,1:T(8,128)(2,1)}, u32[]{:S(2)}, u32[]{:S(2)}) collective-permute-start(bf16[128,768]{0,1:T(8,128)(2,1)} %fusion.187), channel_id=1, source_target_pairs={{0,8},{8,16},{16,24},{24,32},{32,40},{40,48},{48,56},{56,64},{64,7... | collective-permute-start | bytes 589832 | tf_op jit(solution)/shard_map/while/body/eval_jaxpr/ppermute | solution.py:24
  568.5 46.9 %collective-permute-start = (bf16[128,768]{0,1:T(8,128)(2,1)}, bf16[128,768]{0,1:T(8,128)(2,1)}, u32[]{:S(2)}, u32[]{:S(2)}) collective-permute-start(bf16[128,768]{0,1:T(8,128)(2,1)} %copy.159), channel_id=1, source_target_pairs={{0,8},{8,16},{16,24},{24,32},{32,40},{40,48},{48,56},{56,64},{64,7... | collective-permute-start | bytes 589832 | tf_op jit(solution)/shard_map/while/body/eval_jaxpr/ppermute | solution.py:24
  571.8 43.6 %collective-permute-start.1 = (bf16[128,768]{0,1:T(8,128)(2,1)}, bf16[128,768]{0,1:T(8,128)(2,1)}, u32[]{:S(2)}, u32[]{:S(2)}) collective-permute-start(bf16[128,768]{0,1:T(8,128)(2,1)} %copy.160), channel_id=1, source_target_pairs={{0,8},{8,16},{16,24},{24,32},{32,40},{40,48},{48,56},{56,64},{64,7... | collective-permute-start | bytes 589832 | tf_op jit(solution)/shard_map/while/body/eval_jaxpr/ppermute | solution.py:24
  583.3 28.7 %collective-permute-start.2 = (bf16[128,768]{0,1:T(8,128)(2,1)}, bf16[128,768]{0,1:T(8,128)(2,1)}, u32[]{:S(2)}, u32[]{:S(2)}) collective-permute-start(bf16[128,768]{0,1:T(8,128)(2,1)} %fusion.187), channel_id=1, source_target_pairs={{0,8},{8,16},{16,24},{24,32},{32,40},{40,48},{48,56},{56,64},{64,7... | collective-permute-start | bytes 589832 | tf_op jit(solution)/shard_map/while/body/eval_jaxpr/ppermute | solution.py:24
  617.0 46.9 %collective-permute-start = (bf16[128,768]{0,1:T(8,128)(2,1)}, bf16[128,768]{0,1:T(8,128)(2,1)}, u32[]{:S(2)}, u32[]{:S(2)}) collective-permute-start(bf16[128,768]{0,1:T(8,128)(2,1)} %copy.159), channel_id=1, source_target_pairs={{0,8},{8,16},{16,24},{24,32},{32,40},{40,48},{48,56},{56,64},{64,7... | collective-permute-start | bytes 589832 | tf_op jit(solution)/shard_map/while/body/eval_jaxpr/ppermute | solution.py:24
  620.3 43.6 %collective-permute-start.1 = (bf16[128,768]{0,1:T(8,128)(2,1)}, bf16[128,768]{0,1:T(8,128)(2,1)}, u32[]{:S(2)}, u32[]{:S(2)}) collective-permute-start(bf16[128,768]{0,1:T(8,128)(2,1)} %copy.160), channel_id=1, source_target_pairs={{0,8},{8,16},{16,24},{24,32},{32,40},{40,48},{48,56},{56,64},{64,7... | collective-permute-start | bytes 589832 | tf_op jit(solution)/shard_map/while/body/eval_jaxpr/ppermute | solution.py:24
  631.8 28.7 %collective-permute-start.2 = (bf16[128,768]{0,1:T(8,128)(2,1)}, bf16[128,768]{0,1:T(8,128)(2,1)}, u32[]{:S(2)}, u32[]{:S(2)}) collective-permute-start(bf16[128,768]{0,1:T(8,128)(2,1)} %fusion.187), channel_id=1, source_target_pairs={{0,8},{8,16},{16,24},{24,32},{32,40},{40,48},{48,56},{56,64},{64,7... | collective-permute-start | bytes 589832 | tf_op jit(solution)/shard_map/while/body/eval_jaxpr/ppermute | solution.py:24
  665.5 46.9 %collective-permute-start = (bf16[128,768]{0,1:T(8,128)(2,1)}, bf16[128,768]{0,1:T(8,128)(2,1)}, u32[]{:S(2)}, u32[]{:S(2)}) collective-permute-start(bf16[128,768]{0,1:T(8,128)(2,1)} %copy.159), channel_id=1, source_target_pairs={{0,8},{8,16},{16,24},{24,32},{32,40},{40,48},{48,56},{56,64},{64,7... | collective-permute-start | bytes 589832 | tf_op jit(solution)/shard_map/while/body/eval_jaxpr/ppermute | solution.py:24
  668.8 43.6 %collective-permute-start.1 = (bf16[128,768]{0,1:T(8,128)(2,1)}, bf16[128,768]{0,1:T(8,128)(2,1)}, u32[]{:S(2)}, u32[]{:S(2)}) collective-permute-start(bf16[128,768]{0,1:T(8,128)(2,1)} %copy.160), channel_id=1, source_target_pairs={{0,8},{8,16},{16,24},{24,32},{32,40},{40,48},{48,56},{56,64},{64,7... | collective-permute-start | bytes 589832 | tf_op jit(solution)/shard_map/while/body/eval_jaxpr/ppermute | solution.py:24
  680.3 28.7 %collective-permute-start.2 = (bf16[128,768]{0,1:T(8,128)(2,1)}, bf16[128,768]{0,1:T(8,128)(2,1)}, u32[]{:S(2)}, u32[]{:S(2)}) collective-permute-start(bf16[128,768]{0,1:T(8,128)(2,1)} %fusion.187), channel_id=1, source_target_pairs={{0,8},{8,16},{16,24},{24,32},{32,40},{40,48},{48,56},{56,64},{64,7... | collective-permute-start | bytes 589832 | tf_op jit(solution)/shard_map/while/body/eval_jaxpr/ppermute | solution.py:24
  714.0 46.9 %collective-permute-start = (bf16[128,768]{0,1:T(8,128)(2,1)}, bf16[128,768]{0,1:T(8,128)(2,1)}, u32[]{:S(2)}, u32[]{:S(2)}) collective-permute-start(bf16[128,768]{0,1:T(8,128)(2,1)} %copy.159), channel_id=1, source_target_pairs={{0,8},{8,16},{16,24},{24,32},{32,40},{40,48},{48,56},{56,64},{64,7... | collective-permute-start | bytes 589832 | tf_op jit(solution)/shard_map/while/body/eval_jaxpr/ppermute | solution.py:24
  717.3 43.6 %collective-permute-start.1 = (bf16[128,768]{0,1:T(8,128)(2,1)}, bf16[128,768]{0,1:T(8,128)(2,1)}, u32[]{:S(2)}, u32[]{:S(2)}) collective-permute-start(bf16[128,768]{0,1:T(8,128)(2,1)} %copy.160), channel_id=1, source_target_pairs={{0,8},{8,16},{16,24},{24,32},{32,40},{40,48},{48,56},{56,64},{64,7... | collective-permute-start | bytes 589832 | tf_op jit(solution)/shard_map/while/body/eval_jaxpr/ppermute | solution.py:24
  728.8 28.7 %collective-permute-start.2 = (bf16[128,768]{0,1:T(8,128)(2,1)}, bf16[128,768]{0,1:T(8,128)(2,1)}, u32[]{:S(2)}, u32[]{:S(2)}) collective-permute-start(bf16[128,768]{0,1:T(8,128)(2,1)} %fusion.187), channel_id=1, source_target_pairs={{0,8},{8,16},{16,24},{24,32},{32,40},{40,48},{48,56},{56,64},{64,7... | collective-permute-start | bytes 589832 | tf_op jit(solution)/shard_map/while/body/eval_jaxpr/ppermute | solution.py:24
  762.5 46.9 %collective-permute-start = (bf16[128,768]{0,1:T(8,128)(2,1)}, bf16[128,768]{0,1:T(8,128)(2,1)}, u32[]{:S(2)}, u32[]{:S(2)}) collective-permute-start(bf16[128,768]{0,1:T(8,128)(2,1)} %copy.159), channel_id=1, source_target_pairs={{0,8},{8,16},{16,24},{24,32},{32,40},{40,48},{48,56},{56,64},{64,7... | collective-permute-start | bytes 589832 | tf_op jit(solution)/shard_map/while/body/eval_jaxpr/ppermute | solution.py:24
  765.8 43.6 %collective-permute-start.1 = (bf16[128,768]{0,1:T(8,128)(2,1)}, bf16[128,768]{0,1:T(8,128)(2,1)}, u32[]{:S(2)}, u32[]{:S(2)}) collective-permute-start(bf16[128,768]{0,1:T(8,128)(2,1)} %copy.160), channel_id=1, source_target_pairs={{0,8},{8,16},{16,24},{24,32},{32,40},{40,48},{48,56},{56,64},{64,7... | collective-permute-start | bytes 589832 | tf_op jit(solution)/shard_map/while/body/eval_jaxpr/ppermute | solution.py:24
  777.3 28.7 %collective-permute-start.2 = (bf16[128,768]{0,1:T(8,128)(2,1)}, bf16[128,768]{0,1:T(8,128)(2,1)}, u32[]{:S(2)}, u32[]{:S(2)}) collective-permute-start(bf16[128,768]{0,1:T(8,128)(2,1)} %fusion.187), channel_id=1, source_target_pairs={{0,8},{8,16},{16,24},{24,32},{32,40},{40,48},{48,56},{56,64},{64,7... | collective-permute-start | bytes 589832 | tf_op jit(solution)/shard_map/while/body/eval_jaxpr/ppermute | solution.py:24
  811.0 46.9 %collective-permute-start = (bf16[128,768]{0,1:T(8,128)(2,1)}, bf16[128,768]{0,1:T(8,128)(2,1)}, u32[]{:S(2)}, u32[]{:S(2)}) collective-permute-start(bf16[128,768]{0,1:T(8,128)(2,1)} %copy.159), channel_id=1, source_target_pairs={{0,8},{8,16},{16,24},{24,32},{32,40},{40,48},{48,56},{56,64},{64,7... | collective-permute-start | bytes 589832 | tf_op jit(solution)/shard_map/while/body/eval_jaxpr/ppermute | solution.py:24
  814.2 43.6 %collective-permute-start.1 = (bf16[128,768]{0,1:T(8,128)(2,1)}, bf16[128,768]{0,1:T(8,128)(2,1)}, u32[]{:S(2)}, u32[]{:S(2)}) collective-permute-start(bf16[128,768]{0,1:T(8,128)(2,1)} %copy.160), channel_id=1, source_target_pairs={{0,8},{8,16},{16,24},{24,32},{32,40},{40,48},{48,56},{56,64},{64,7... | collective-permute-start | bytes 589832 | tf_op jit(solution)/shard_map/while/body/eval_jaxpr/ppermute | solution.py:24
  825.8 28.7 %collective-permute-start.2 = (bf16[128,768]{0,1:T(8,128)(2,1)}, bf16[128,768]{0,1:T(8,128)(2,1)}, u32[]{:S(2)}, u32[]{:S(2)}) collective-permute-start(bf16[128,768]{0,1:T(8,128)(2,1)} %fusion.187), channel_id=1, source_target_pairs={{0,8},{8,16},{16,24},{24,32},{32,40},{40,48},{48,56},{56,64},{64,7... | collective-permute-start | bytes 589832 | tf_op jit(solution)/shard_map/while/body/eval_jaxpr/ppermute | solution.py:24
  859.5 46.9 %collective-permute-start = (bf16[128,768]{0,1:T(8,128)(2,1)}, bf16[128,768]{0,1:T(8,128)(2,1)}, u32[]{:S(2)}, u32[]{:S(2)}) collective-permute-start(bf16[128,768]{0,1:T(8,128)(2,1)} %copy.159), channel_id=1, source_target_pairs={{0,8},{8,16},{16,24},{24,32},{32,40},{40,48},{48,56},{56,64},{64,7... | collective-permute-start | bytes 589832 | tf_op jit(solution)/shard_map/while/body/eval_jaxpr/ppermute | solution.py:24
  862.7 43.6 %collective-permute-start.1 = (bf16[128,768]{0,1:T(8,128)(2,1)}, bf16[128,768]{0,1:T(8,128)(2,1)}, u32[]{:S(2)}, u32[]{:S(2)}) collective-permute-start(bf16[128,768]{0,1:T(8,128)(2,1)} %copy.160), channel_id=1, source_target_pairs={{0,8},{8,16},{16,24},{24,32},{32,40},{40,48},{48,56},{56,64},{64,7... | collective-permute-start | bytes 589832 | tf_op jit(solution)/shard_map/while/body/eval_jaxpr/ppermute | solution.py:24
  874.3 28.7 %collective-permute-start.2 = (bf16[128,768]{0,1:T(8,128)(2,1)}, bf16[128,768]{0,1:T(8,128)(2,1)}, u32[]{:S(2)}, u32[]{:S(2)}) collective-permute-start(bf16[128,768]{0,1:T(8,128)(2,1)} %fusion.187), channel_id=1, source_target_pairs={{0,8},{8,16},{16,24},{24,32},{32,40},{40,48},{48,56},{56,64},{64,7... | collective-permute-start | bytes 589832 | tf_op jit(solution)/shard_map/while/body/eval_jaxpr/ppermute | solution.py:24
  908.0 46.9 %collective-permute-start = (bf16[128,768]{0,1:T(8,128)(2,1)}, bf16[128,768]{0,1:T(8,128)(2,1)}, u32[]{:S(2)}, u32[]{:S(2)}) collective-permute-start(bf16[128,768]{0,1:T(8,128)(2,1)} %copy.159), channel_id=1, source_target_pairs={{0,8},{8,16},{16,24},{24,32},{32,40},{40,48},{48,56},{56,64},{64,7... | collective-permute-start | bytes 589832 | tf_op jit(solution)/shard_map/while/body/eval_jaxpr/ppermute | solution.py:24
  911.2 43.6 %collective-permute-start.1 = (bf16[128,768]{0,1:T(8,128)(2,1)}, bf16[128,768]{0,1:T(8,128)(2,1)}, u32[]{:S(2)}, u32[]{:S(2)}) collective-permute-start(bf16[128,768]{0,1:T(8,128)(2,1)} %copy.160), channel_id=1, source_target_pairs={{0,8},{8,16},{16,24},{24,32},{32,40},{40,48},{48,56},{56,64},{64,7... | collective-permute-start | bytes 589832 | tf_op jit(solution)/shard_map/while/body/eval_jaxpr/ppermute | solution.py:24
  922.8 28.7 %collective-permute-start.2 = (bf16[128,768]{0,1:T(8,128)(2,1)}, bf16[128,768]{0,1:T(8,128)(2,1)}, u32[]{:S(2)}, u32[]{:S(2)}) collective-permute-start(bf16[128,768]{0,1:T(8,128)(2,1)} %fusion.187), channel_id=1, source_target_pairs={{0,8},{8,16},{16,24},{24,32},{32,40},{40,48},{48,56},{56,64},{64,7... | collective-permute-start | bytes 589832 | tf_op jit(solution)/shard_map/while/body/eval_jaxpr/ppermute | solution.py:24
  956.5 46.9 %collective-permute-start = (bf16[128,768]{0,1:T(8,128)(2,1)}, bf16[128,768]{0,1:T(8,128)(2,1)}, u32[]{:S(2)}, u32[]{:S(2)}) collective-permute-start(bf16[128,768]{0,1:T(8,128)(2,1)} %copy.159), channel_id=1, source_target_pairs={{0,8},{8,16},{16,24},{24,32},{32,40},{40,48},{48,56},{56,64},{64,7... | collective-permute-start | bytes 589832 | tf_op jit(solution)/shard_map/while/body/eval_jaxpr/ppermute | solution.py:24
  959.7 43.6 %collective-permute-start.1 = (bf16[128,768]{0,1:T(8,128)(2,1)}, bf16[128,768]{0,1:T(8,128)(2,1)}, u32[]{:S(2)}, u32[]{:S(2)}) collective-permute-start(bf16[128,768]{0,1:T(8,128)(2,1)} %copy.160), channel_id=1, source_target_pairs={{0,8},{8,16},{16,24},{24,32},{32,40},{40,48},{48,56},{56,64},{64,7... | collective-permute-start | bytes 589832 | tf_op jit(solution)/shard_map/while/body/eval_jaxpr/ppermute | solution.py:24
  971.3 28.7 %collective-permute-start.2 = (bf16[128,768]{0,1:T(8,128)(2,1)}, bf16[128,768]{0,1:T(8,128)(2,1)}, u32[]{:S(2)}, u32[]{:S(2)}) collective-permute-start(bf16[128,768]{0,1:T(8,128)(2,1)} %fusion.187), channel_id=1, source_target_pairs={{0,8},{8,16},{16,24},{24,32},{32,40},{40,48},{48,56},{56,64},{64,7... | collective-permute-start | bytes 589832 | tf_op jit(solution)/shard_map/while/body/eval_jaxpr/ppermute | solution.py:24
  1005.0 47.1 %collective-permute-start = (bf16[128,768]{0,1:T(8,128)(2,1)}, bf16[128,768]{0,1:T(8,128)(2,1)}, u32[]{:S(2)}, u32[]{:S(2)}) collective-permute-start(bf16[128,768]{0,1:T(8,128)(2,1)} %copy.159), channel_id=1, source_target_pairs={{0,8},{8,16},{16,24},{24,32},{32,40},{40,48},{48,56},{56,64},{64,7... | collective-permute-start | bytes 589832 | tf_op jit(solution)/shard_map/while/body/eval_jaxpr/ppermute | solution.py:24
  1008.2 43.8 %collective-permute-start.1 = (bf16[128,768]{0,1:T(8,128)(2,1)}, bf16[128,768]{0,1:T(8,128)(2,1)}, u32[]{:S(2)}, u32[]{:S(2)}) collective-permute-start(bf16[128,768]{0,1:T(8,128)(2,1)} %copy.160), channel_id=1, source_target_pairs={{0,8},{8,16},{16,24},{24,32},{32,40},{40,48},{48,56},{56,64},{64,7... | collective-permute-start | bytes 589832 | tf_op jit(solution)/shard_map/while/body/eval_jaxpr/ppermute | solution.py:24
  1017.9 30.7 %collective-permute-start.2 = (bf16[128,768]{0,1:T(8,128)(2,1)}, bf16[128,768]{0,1:T(8,128)(2,1)}, u32[]{:S(2)}, u32[]{:S(2)}) collective-permute-start(bf16[128,768]{0,1:T(8,128)(2,1)} %fusion.187), channel_id=1, source_target_pairs={{0,8},{8,16},{16,24},{24,32},{32,40},{40,48},{48,56},{56,64},{64,7... | collective-permute-start | bytes 589832 | tf_op jit(solution)/shard_map/while/body/eval_jaxpr/ppermute | solution.py:24
  1073.8 594.7 %reduce-scatter.7.cloned.1.call-start = ((), (), s32[]{:S(2)}) async-start(), calls=%async_computation.7 | async-start | bytes 5013504 | tf_op jit(solution)/shard_map/reduce_scatter | solution.py:365
  1079.7 590.6 %reduce-scatter.5.cloned.1.call-start = ((), (), s32[]{:S(2)}) async-start(), calls=%async_computation.6 | async-start | bytes 5013504 | tf_op jit(solution)/shard_map/reduce_scatter | solution.py:362
  1437.8 29.0 %collective-permute-start.34 = (f32[8,768]{1,0:T(8,128)}, f32[8,768]{1,0:T(8,128)}, u32[]{:S(2)}, u32[]{:S(2)}) collective-permute-start(f32[8,768]{1,0:T(8,128)} %fusion), channel_id=1, source_target_pairs={{0,31},{1,32},{2,33},{3,34},{4,35},{5,36},{6,37},{7,38},{8,39},{9,... | collective-permute-start | bytes 73736
  1440.4 23.0 %collective-permute-start.35 = (f32[6,768]{1,0:T(8,128)S(1)}, f32[6,768]{1,0:T(8,128)S(1)}, u32[]{:S(2)}, u32[]{:S(2)}) collective-permute-start(f32[6,768]{1,0:T(8,128)S(1)} %slice.31), channel_id=1, source_target_pairs={{0,32},{1,33},{2,34},{3,35},{4,36},{5,37},{6,38},{7,39},{8,40},{9,... | collective-permute-start | bytes 55304
  1441.7 27.0 %collective-permute-start.33 = (f32[8,768]{1,0:T(8,128)}, f32[8,768]{1,0:T(8,128)}, u32[]{:S(2)}, u32[]{:S(2)}) collective-permute-start(f32[8,768]{1,0:T(8,128)} %fusion), channel_id=1, source_target_pairs={{0,30},{1,31},{2,32},{3,33},{4,34},{5,35},{6,36},{7,37},{8,38},{9,... | collective-permute-start | bytes 73736
  1443.6 26.4 %collective-permute-start.32 = (f32[8,768]{1,0:T(8,128)}, f32[8,768]{1,0:T(8,128)}, u32[]{:S(2)}, u32[]{:S(2)}) collective-permute-start(f32[8,768]{1,0:T(8,128)} %fusion), channel_id=1, source_target_pairs={{0,29},{1,30},{2,31},{3,32},{4,33},{5,34},{6,35},{7,36},{8,37},{9,... | collective-permute-start | bytes 73736
  1446.3 25.0 %collective-permute-start.31 = (f32[8,768]{1,0:T(8,128)}, f32[8,768]{1,0:T(8,128)}, u32[]{:S(2)}, u32[]{:S(2)}) collective-permute-start(f32[8,768]{1,0:T(8,128)} %fusion), channel_id=1, source_target_pairs={{0,28},{1,29},{2,30},{3,31},{4,32},{5,33},{6,34},{7,35},{8,36},{9,... | collective-permute-start | bytes 73736
  1510.6 82.8 %collective-permute-start.13 = (f32[8,768]{1,0:T(8,128)}, f32[8,768]{1,0:T(8,128)}, u32[]{:S(2)}, u32[]{:S(2)}) collective-permute-start(f32[8,768]{1,0:T(8,128)} %fusion), channel_id=1, source_target_pairs={{0,10},{1,11},{2,12},{3,13},{4,14},{5,15},{6,16},{7,17},{8,18},{9,... | collective-permute-start | bytes 73736
  1512.5 85.7 %collective-permute-start.12 = (f32[8,768]{1,0:T(8,128)}, f32[8,768]{1,0:T(8,128)}, u32[]{:S(2)}, u32[]{:S(2)}) collective-permute-start(f32[8,768]{1,0:T(8,128)} %fusion), channel_id=1, source_target_pairs={{0,9},{1,10},{2,11},{3,12},{4,13},{5,14},{6,15},{7,16},{8,17},{9,1... | collective-permute-start | bytes 73736
  1517.6 83.4 %collective-permute-start.11 = (f32[8,768]{1,0:T(8,128)}, f32[8,768]{1,0:T(8,128)}, u32[]{:S(2)}, u32[]{:S(2)}) collective-permute-start(f32[8,768]{1,0:T(8,128)} %fusion), channel_id=1, source_target_pairs={{0,8},{1,9},{2,10},{3,11},{4,12},{5,13},{6,14},{7,15},{8,16},{9,17... | collective-permute-start | bytes 73736
  1519.5 84.4 %collective-permute-start.10 = (f32[8,768]{1,0:T(8,128)}, f32[8,768]{1,0:T(8,128)}, u32[]{:S(2)}, u32[]{:S(2)}) collective-permute-start(f32[8,768]{1,0:T(8,128)} %fusion), channel_id=1, source_target_pairs={{0,7},{1,8},{2,9},{3,10},{4,11},{5,12},{6,13},{7,14},{8,15},{9,16}... | collective-permute-start | bytes 73736
  1522.4 86.9 %collective-permute-start.9 = (f32[8,768]{1,0:T(8,128)}, f32[8,768]{1,0:T(8,128)}, u32[]{:S(2)}, u32[]{:S(2)}) collective-permute-start(f32[8,768]{1,0:T(8,128)} %fusion), channel_id=1, source_target_pairs={{0,6},{1,7},{2,8},{3,9},{4,10},{5,11},{6,12},{7,13},{8,14},{9,15},... | collective-permute-start | bytes 73736
  1593.4 22.6 %collective-permute-start.8 = (f32[8,768]{1,0:T(8,128)}, f32[8,768]{1,0:T(8,128)}, u32[]{:S(2)}, u32[]{:S(2)}) collective-permute-start(f32[8,768]{1,0:T(8,128)} %fusion), channel_id=1, source_target_pairs={{0,5},{1,6},{2,7},{3,8},{4,9},{5,10},{6,11},{7,12},{8,13},{9,14},{... | collective-permute-start | bytes 73736
  (215 other events, 3736.2 us)
Sparse Core Ops, SparseCore 0:
  12.0 39.2 all-gather.6
  53.0 35.9 all-gather.4
  1073.9 169.3 all-reduce.8
  1245.5 69.7 reduce-scatter.6
  1317.6 78.1 reduce-scatter.4
where the time goes:
time: 1690 us; the launch traced here: 1680 us
  starting transfers between devices  425 us (25%)
  blocking collectives  416 us (25%)
  local copies, waits for them, and re-layouts  291 us (17%)
  other arithmetic  254 us (15%)
  matrix products  182 us (11%)
  waiting for transfers between devices  92.9 us (5%)
    unnamed x2, blocking collectives  416 us
    ppermute x64, starting transfers between devices, from_behind(): return lax.ppermute(value, axis, pairs)  306 us
    unnamed x33, starting transfers between devices  99.4 us
    while x300, local copies, waits for them, and re-layouts  69.9 us
    another operation x48, local copies, waits for them, and re-layouts  64 us
    unnamed x94, local copies, waits for them, and re-layouts  62.8 us
    convert_element_type x32, other arithmetic, turn(): part.astype(own.dtype)  54.3 us
    all_gather x1, waiting for transfers between devices, body(): lax.all_gather(keys, 'ctx', axis=0, tiled=True)  37.7 us
  transfers between devices with their start and end apart: 105, of which 7 were waited for; matrix products, arithmetic and copies ran while one was open for 52% of the time, Pallas kernels for 0%

commit v1 on v0

v1 whole, which is shorter than its diff:
```python
import jax
import jax.numpy as jnp
import numpy as np
from jax import lax
from jax.experimental import pallas as pl
from jax.experimental.pallas import tpu as pltpu
from jax.sharding import PartitionSpec as P

HEADS = 12
HEAD_DIM = 64
BUCKETS = 32
MAX_DISTANCE = 128
EPSILON = 1e-06
SCALE = HEAD_DIM ** (-0.5)
TOK = 128
WIDTH = 768
FF = 3072
CAP = 24
F32 = jnp.float32
BF16 = jnp.bfloat16
MESH = pl.DeviceIdType.MESH
VMEM = pl.BlockSpec(memory_space=pltpu.VMEM)
SMEM = pl.BlockSpec(memory_space=pltpu.SMEM)
ANY = pl.BlockSpec(memory_space=pl.ANY)
VMEM_LIMIT = 60 * 1024 * 1024


def bucket_edges(buckets, reach):
    half = buckets // 2
    exact = half // 2
    spans = np.arange(1, reach + 1)
    spread = np.log(np.maximum(spans, exact) / exact) / np.log(reach / exact) * (half - exact)
    large = np.minimum(exact + spread.astype(np.int64), half - 1)
    level = np.where(spans < exact, spans, large)
    return [int(np.argmax(level >= b)) + 1 for b in range(1, half)]


EDGES = bucket_edges(BUCKETS, MAX_DISTANCE)


def dot(a, b):
    return jnp.dot(a, b, preferred_element_type=F32)


def dot_nt(a, b):
    return lax.dot_general(a, b, (((1,), (1,)), ((), ())), preferred_element_type=F32)


def dot_tn(a, b):
    return lax.dot_general(a, b, (((0,), (0,)), ((), ())), preferred_element_type=F32)


def iota(shape, dim):
    return lax.broadcasted_iota(jnp.int32, shape, dim)


class Place:
    def __init__(self):
        self.i = lax.axis_index("ctx")
        self.e = lax.axis_index("expert")
        self.x = lax.div(self.i, 4)
        self.y = lax.rem(lax.div(self.i, 2), 2)
        self.c = lax.rem(self.i, 2)
        self.z = lax.div(self.e, 2)
        self.h = lax.rem(self.e, 2)
        self.q = self.h * 2 + self.y

    def x_of(self, step):
        return lax.rem(self.x + 4 + step, 4)

    def x_peer(self, step):
        return (4 * self.x_of(step) + 2 * self.y + self.c, self.e)

    def core_peer(self):
        return (4 * self.x + 2 * self.y + 1 - self.c, self.e)

    def y_peer(self):
        return (4 * self.x + 2 * (1 - self.y) + self.c, self.e)

    def z_of(self, step):
        return lax.rem(self.z + 4 + step, 4)

    def z_peer(self, step):
        return (self.i, 2 * self.z_of(step) + self.h)

    def q_of(self, step):
        return lax.rem(self.q + 4 + step, 4)

    def q_peer(self, step):
        q = self.q_of(step)
        return (4 * self.x + 2 * lax.rem(q, 2) + self.c, 2 * self.z + lax.div(q, 2))

    def e_of(self, step):
        return lax.rem(self.e + 8 + step, 8)

    def e_peer(self, step):
        return (self.i, self.e_of(step))


def greet(peers):
    barrier = pltpu.get_barrier_semaphore()
    for peer in peers:
        pl.semaphore_signal(barrier, inc=1, device_id=peer, device_id_type=MESH)
    pl.semaphore_wait(barrier, len(peers))


def rcopy(src, dst, send, recv, slot, peer):
    return pltpu.make_async_remote_copy(
        src_ref=src,
        dst_ref=dst,
        send_sem=send.at[slot],
        recv_sem=recv.at[slot],
        device_id=peer,
        device_id_type=MESH,
    )


def rows(index, size):
    return pl.ds(pl.multiple_of(index * size, size), size)


def pair(first, half_first, second, half_second):
    if first is second and (half_first, half_second) == (0, 1):
        return first
    low = pltpu.roll(first, 64, 1) if half_first else first
    high = second if half_second else pltpu.roll(second, 64, 1)
    return jnp.where(iota(low.shape, 1) < 64, low, high)


def norm_places():
    col = iota((1, 1024), 1)
    r = col & 7
    xx = (col >> 3) & 3
    yl = (col >> 5) & 1
    e = (((col >> 7) & 3) << 1) + ((col >> 6) & 1)
    c = (col >> 9) & 1
    d = jnp.where(r < 6, 192 * xx + 96 * yl + 48 * c + 6 * e + r, -1)
    return (iota((WIDTH, 1024), 0) == d).astype(F32).astype(BF16)


def out_places():
    col = iota((1, 1024), 1)
    r = col & 7
    xx = (col >> 3) & 3
    yl = (col >> 5) & 1
    e = (((col >> 7) & 3) << 1) + ((col >> 6) & 1)
    c = (col >> 9) & 1
    f = 96 * yl + 48 * c + 6 * e + 2 * xx + r - 6
    f = jnp.where((r >= 6) & (xx < 3), f, -1)
    lane = iota((256, 1024), 0)
    feature = jnp.where(lane >= 128, lane - 128, jnp.where(lane >= 64, lane + 64, -2))
    return (feature == f).astype(F32).astype(BF16)


def bucket_tile(offset):
    length = jnp.abs(offset)
    level = jnp.where(offset > 0, BUCKETS // 2, 0)
    for edge in EDGES:
        level = level + (length >= edge).astype(jnp.int32)
    return level


def forward_kernel(
    inp_ref, gain_ref, w_ref, table_ref,
    att_ref, own_ref, q_ref, kv_ref, p_ref, inv_ref, norm_ref,
    proj, q_send, kv_send, norm_send, qexp, bias, s_ref, m_ref, l_ref, acc, o_t, send, recv,
):
    me = Place()
    greet([me.x_peer(1), me.x_peer(2), me.x_peer(3), me.core_peer(), me.y_peer()])
    inputs = inp_ref[...].astype(F32)
    root = lax.rsqrt(jnp.mean(inputs * inputs, axis=1, keepdims=True) + EPSILON)
    normed = (inputs * root * gain_ref[...]).astype(BF16)
    for p in range(3):
        proj[p] = dot(normed, w_ref[p])

    def group(p, piece):
        return proj[p, :, pl.ds(128 * (piece // 2), 128)]

    def join(p, a, s, b):
        first = group(p, a)
        second = first if (p == s and a // 2 == b // 2) else group(s, b)
        return pair(first, a % 2, second, b % 2)

    lane = iota((TOK, 128), 1)
    for g in range(4):
        a = 3 * g
        kv_send[g, :, pl.ds(0, 128)] = join(1, a, 1, a + 1).astype(BF16)
        kv_send[g, :, pl.ds(128, 128)] = join(1, a + 2, 2, a + 2).astype(BF16)
        kv_send[g, :, pl.ds(256, 128)] = join(2, a, 2, a + 1).astype(BF16)
        q_send[g, :, pl.ds(0, 128)] = join(0, a, 0, a + 1).astype(BF16)
        q_send[g, :, pl.ds(128, 128)] = jnp.where(lane < 64, join(0, a + 2, 0, a + 2), 0.0).astype(BF16)
    block = rows(me.i, TOK)
    copies = {}
    for step in (1, 3, 2):
        peer = me.x_peer(step)
        copies["kv", step] = rcopy(kv_send.at[me.x_of(step)], kv_ref.at[block], send, recv, step, peer)
        copies["kv", step].start()
    for step in (1, 3, 2):
        copies["q", step] = rcopy(
            q_send.at[me.x_of(step)], q_ref.at[rows(me.x, TOK)], send, recv, 4 + step, me.x_peer(step)
        )
        copies["q", step].start()
    kv_ref[block, :] = kv_send[me.x]
    q_ref[rows(me.x, TOK), :] = q_send[me.x]

    def source(step, y, c):
        return rows(4 * me.x_of(-step) + 2 * y + c, TOK)

    def pass_on(step):
        part = kv_ref.at[source(step, me.y, me.c)]
        copies["y", step] = rcopy(part, part, send, recv, 8 + step, me.y_peer())
        copies["y", step].start()
        copies["c", step] = rcopy(part, part, send, recv, 12 + step, me.core_peer())
        copies["c", step].start()

    pass_on(0)
    normed_wide = dot(normed, norm_places()).astype(BF16)
    norm_send[...] = normed_wide
    norm_ref[rows(me.x, TOK), :] = normed_wide
    tile = iota((128, 128), 0) - iota((128, 128), 1)
    for h in range(3):
        head = 3 * me.x + h

        def chain(first, n):
            value = jnp.full((128, 128), 1.0, F32) * table_ref[first, head]
            for level, edge in enumerate(EDGES):
                value = jnp.where(n >= edge, table_ref[first + level + 1, head], value)
            return value

        bias[h, 0] = jnp.full((128, 128), 1.0, F32) * table_ref[BUCKETS // 2 - 1, head]
        bias[h, 1] = chain(0, 128 - tile)
        bias[h, 2] = jnp.where(tile > 0, chain(BUCKETS // 2, tile), chain(0, -tile))
        bias[h, 3] = chain(BUCKETS // 2, 128 + tile)
        bias[h, 4] = jnp.full((128, 128), 1.0, F32) * table_ref[BUCKETS - 1, head]
        m_ref[h] = jnp.full((8, 512), -jnp.inf, F32)
        l_ref[h] = jnp.zeros((8, 512), F32)
    for step in (1, 3, 2):
        copies["q", step].wait_recv()
    lanes = iota((512, 256), 1)
    for h in range(3):
        mine = (lanes >= 64 * h) & (lanes < 64 * h + 64)
        qexp[h] = jnp.where(mine, q_ref[...].astype(F32) * SCALE, 0.0).astype(BF16)

    def score_blocks(first, last, y, c):
        def one(step, carry):
            b = 4 * me.x_of(-step) + 2 * y + c
            keys = kv_ref[rows(b, TOK), pl.ds(0, 256)]
            for h in range(3):
                s = dot_nt(keys, qexp[h])
                for t in range(4):
                    kind = jnp.clip(b - (4 * t + 2 * me.y + me.c), -2, 2) + 2
                    part = s[:, 128 * t : 128 * t + 128] + bias[h, kind]
                    cols = pl.ds(128 * t, 128)
                    s_ref[h, rows(b, TOK), cols] = part
                    m_ref[h, :, cols] = jnp.maximum(m_ref[h, :, cols], jnp.max(part.reshape(16, 8, 128), axis=0))
            return carry

        lax.fori_loop(first, last, one, 0)

    score_blocks(0, 1, me.y, me.c)
    for step in (1, 3, 2):
        copies["kv", step].wait_recv()
        pass_on(step)
    score_blocks(1, 4, me.y, me.c)
    for step in (0, 1, 3, 2):
        copies["y", step].wait_recv()
        part = kv_ref.at[source(step, 1 - me.y, me.c)]
        copies["f", step] = rcopy(part, part, send, recv, 16 + step, me.core_peer())
        copies["f", step].start()
        if step == 2:
            for other in (1, 3, 2):
                copies["n", other] = rcopy(
                    norm_send, norm_ref.at[rows(me.x, TOK)], send, recv, 20 + other, me.x_peer(other)
                )
                copies["n", other].start()
    for step in range(4):
        copies["c", step].wait_recv()
    score_blocks(0, 4, me.y, 1 - me.c)
    score_blocks(0, 4, 1 - me.y, me.c)
    for step in range(4):
        copies["f", step].wait_recv()
    score_blocks(0, 4, 1 - me.y, 1 - me.c)
    o_t[...] = jnp.zeros_like(o_t)
    inv_rows = jnp.zeros((128, 512), F32)
    for h in range(3):
        top = jnp.max(m_ref[h], axis=0, keepdims=True)
        acc[...] = jnp.zeros_like(acc)

        def weigh(j, carry):
            part = jnp.exp(s_ref[h, rows(j, 256), :] - top)
            l_ref[h] += jnp.sum(part.reshape(32, 8, 512), axis=0)
            low = part.astype(BF16)
            p_ref[rows(j, 256), pl.ds(512 * h, 512)] = low
            acc[...] += dot_tn(kv_ref[rows(j, 256), pl.ds(128, 256)], low)
            return carry

        lax.fori_loop(0, 8, weigh, 0)
        inv = 1.0 / jnp.sum(l_ref[h], axis=0, keepdims=True)
        at = (128, 192, 64)[h]
        o_t[pl.ds(at, 64), :] = acc[pl.ds(at, 64), :] * inv
        inv_rows = jnp.where(iota((128, 512), 0) == h, inv, inv_rows)
    inv_ref[...] = inv_rows.T
    own_ref[...] = o_t[...].T.astype(BF16)
    for step in (1, 3, 2):
        copies["o", step] = rcopy(
            own_ref.at[rows(me.x_of(step), TOK)], att_ref.at[me.x], send, recv, 24 + step, me.x_peer(step)
        )
        copies["o", step].start()
    att_ref[me.x] = own_ref[rows(me.x, TOK), :]
    for step in (1, 3, 2):
        copies["n", step].wait_recv()
        copies["o", step].wait_recv()
    for copy in copies.values():
        copy.wait_send()


def forward(inputs, gain, weights, table):
    shape = jax.ShapeDtypeStruct
    return pl.pallas_call(
        forward_kernel,
        out_shape=(
            shape((4, TOK, 256), BF16),
            shape((512, 256), BF16),
            shape((512, 256), BF16),
            shape((2048, 384), BF16),
            shape((2048, 1536), BF16),
            shape((512, 128), F32),
            shape((512, 1024), BF16),
        ),
        in_specs=[VMEM, VMEM, VMEM, SMEM],
        out_specs=(VMEM,) * 7,
        scratch_shapes=[
            pltpu.VMEM((3, TOK, WIDTH), F32),
            pltpu.VMEM((4, TOK, 256), BF16),
            pltpu.VMEM((4, TOK, 384), BF16),
            pltpu.VMEM((TOK, 1024), BF16),
            pltpu.VMEM((3, 512, 256), BF16),
            pltpu.VMEM((3, 5, 128, 128), F32),
            pltpu.VMEM((3, 2048, 512), F32),
            pltpu.VMEM((3, 8, 512), F32),
            pltpu.VMEM((3, 8, 512), F32),
            pltpu.VMEM((256, 512), F32),
            pltpu.VMEM((256, 512), F32),
            pltpu.SemaphoreType.DMA((28,)),
            pltpu.SemaphoreType.DMA((28,)),
        ],
        compiler_params=pltpu.CompilerParams(
            collective_id=0, has_side_effects=True, vmem_limit_bytes=VMEM_LIMIT
        ),
    )(inputs, gain, weights, table)


def expert_kernel(
    att_ref, inp_ref, out_w_ref, gain_ref, router_ref, routes_ref, w_in_hbm, w_out_hbm, cot_ref,
    y_ref, gmid_ref, gmix_ref, small_ref, da_ref, gwi_hbm, gwo_hbm,
    w_in, w_out, middle, select, send_rows, recv_rows, send_back, recv_back, hidden, ginner,
    arrived, gprod, made, garr, gwi, gwo, da_send, local, send, recv,
):
    me = Place()
    load_in = pltpu.make_async_copy(w_in_hbm.at[0], w_in, local.at[0])
    load_in.start()
    load_out = pltpu.make_async_copy(w_out_hbm.at[0], w_out, local.at[1])
    load_out.start()
    greet([me.e_peer(k) for k in range(1, 8)] + [me.x_peer(k) for k in range(1, 4)])
    mixed = inp_ref[...].astype(F32)
    for g in range(4):
        mixed = mixed + dot(att_ref[g, :, pl.ds(0, 128)], out_w_ref[pl.ds(192 * g + 64, 128), :])
        mixed = mixed + dot(att_ref[g, :, pl.ds(128, 128)], out_w_ref[pl.ds(192 * g, 128), :])
    middle[...] = mixed
    root = lax.rsqrt(jnp.mean(mixed * mixed, axis=1, keepdims=True) + EPSILON)
    normed = (mixed * root * gain_ref[...]).astype(BF16)
    logits = dot(normed, router_ref[...])
    shifted = jnp.exp(logits - jnp.max(logits, axis=1, keepdims=True))
    router = shifted / jnp.sum(shifted, axis=1, keepdims=True)
    choose = routes_ref[...] == iota((TOK, 8), 1)
    chosen = choose.astype(F32)
    gate = jnp.sum(chosen * router, axis=1, keepdims=True)
    earlier = (iota((TOK, TOK), 0) > iota((TOK, TOK), 1)).astype(F32).astype(BF16)
    ranks = dot(earlier, chosen.astype(BF16))
    slot = jnp.sum(chosen * ranks, axis=1, keepdims=True).astype(jnp.int32)
    target = routes_ref[...] * (2 * CAP) + slot
    column = iota((TOK, 16 * CAP), 1)
    select[pl.ds(0, TOK), :] = (column == target).astype(F32).astype(BF16)
    select[pl.ds(TOK, TOK), :] = (column == target + CAP).astype(F32).astype(BF16)
    dy = cot_ref[...].astype(F32)
    both = jnp.concatenate([normed, (gate * dy).astype(BF16)], axis=0)
    send_rows[...] = dot_tn(select[...], both).astype(BF16)
    mine = rows(me.e, 2 * CAP)
    there = []
    for k in (1, 7, 2, 6, 3, 5, 4):
        copy = rcopy(
            send_rows.at[rows(me.e_of(k), 2 * CAP)], recv_rows.at[mine], send, recv, k, me.e_peer(k)
        )
        copy.start()
        there.append(copy)
    recv_rows[mine, :] = send_rows[mine, :]
    made[...] = jnp.zeros_like(made)
    garr[...] = jnp.zeros_like(garr)
    load_in.wait()
    load_out.wait()
    for copy in there:
        copy.wait_recv()
    got = recv_rows[...].astype(F32).reshape(8, 2 * CAP, WIDTH)
    arrived[...] = got[:, :CAP].reshape(8 * CAP, WIDTH).astype(BF16)
    gprod[...] = got[:, CAP:].reshape(8 * CAP, WIDTH).astype(BF16)
    chunk = 512

    def through(j, carry):
        cols = rows(j, chunk)
        inner = dot(arrived[...], w_in[:, cols])
        square = inner * inner
        slope = np.float32(np.sqrt(2 / np.pi))
        t = jnp.tanh(slope * inner * (1.0 + 0.044715 * square))
        half = 0.5 * (1.0 + t)
        low = (inner * half).astype(BF16)
        hidden[:, cols] = low
        made[...] += dot(low, w_out[cols, :])
        back = dot_nt(gprod[...], w_out[cols, :])
        lean = half + 0.5 * inner * (1.0 - t * t) * slope * (1.0 + 3 * 0.044715 * square)
        grad = (lean * back).astype(BF16)
        ginner[:, cols] = grad
        garr[...] += dot_nt(grad, w_in[:, cols])
        return carry

    lax.fori_loop(0, FF // chunk, through, 0)
    back = jnp.concatenate([made[...].reshape(8, CAP, WIDTH), garr[...].reshape(8, CAP, WIDTH)], axis=1)
    send_back[...] = back.reshape(16 * CAP, WIDTH).astype(BF16)
    home = []
    for k in (1, 7, 2, 6, 3, 5, 4):
        copy = rcopy(
            send_back.at[rows(me.e_of(k), 2 * CAP)], recv_back.at[mine], send, recv, 8 + k, me.e_peer(k)
        )
        copy.start()
        home.append(copy)
    recv_back[mine, :] = send_back[mine, :]

    def weight_grads(j, carry):
        cols = rows(j, chunk)
        gwo[cols, :] = dot_tn(hidden[:, cols], gprod[...]).astype(BF16)
        gwi[:, cols] = dot_tn(arrived[...], ginner[:, cols]).astype(BF16)
        return carry

    lax.fori_loop(0, FF // chunk, weight_grads, 0)
    keep_in = pltpu.make_async_copy(gwi, gwi_hbm, local.at[2])
    keep_in.start()
    keep_out = pltpu.make_async_copy(gwo, gwo_hbm, local.at[3])
    keep_out.start()
    for copy in home:
        copy.wait_recv()
    returned = dot(select[pl.ds(0, TOK), :], recv_back[...])
    gnorm = dot(select[pl.ds(TOK, TOK), :], recv_back[...])
    mid = middle[...]
    y_ref[...] = (mid + gate * returned).astype(BF16)
    ggate = jnp.sum(dy * returned, axis=1, keepdims=True)
    glogits = ggate * gate * (chosen - router)
    high = glogits.astype(BF16)
    rest = (glogits - high.astype(F32)).astype(BF16)
    gnorm = gnorm + dot_nt(high, router_ref[...]) + dot_nt(rest, router_ref[...])
    small_ref[...] = jnp.zeros_like(small_ref)
    small_ref[pl.ds(8, 8), :] = dot_tn(high, normed) + dot_tn(rest, normed)
    small_ref[pl.ds(1, 1), :] = jnp.sum(gnorm * mid * root, axis=0, keepdims=True)
    u = gain_ref[...] * gnorm
    gmid = dy + root * u - mid * (root * root * root * jnp.mean(u * mid, axis=1, keepdims=True))
    gmid_ref[...] = gmid
    gmix = gmid.astype(BF16)
    gmix_ref[...] = gmix
    upper = iota((TOK, 128), 1) >= 64
    for g in range(4):
        front = dot_nt(gmix, out_w_ref[pl.ds(192 * g + 64, 128), :])
        da_send[g, :, pl.ds(0, 128)] = jnp.where(upper, front, 0.0).astype(BF16)
        da_send[g, :, pl.ds(128, 128)] = dot_nt(gmix, out_w_ref[pl.ds(192 * g, 128), :]).astype(BF16)
    away = []
    for k in (1, 3, 2):
        copy = rcopy(da_send.at[me.x_of(k)], da_ref.at[rows(me.x, TOK)], send, recv, 16 + k, me.x_peer(k))
        copy.start()
        away.append(copy)
    da_ref[rows(me.x, TOK), :] = da_send[me.x]
    for copy in away:
        copy.wait_recv()
    for copy in there + home + away:
        copy.wait_send()
    keep_in.wait()
    keep_out.wait()


def expert(att, inputs, out_w, gain, router_w, routes, w_in, w_out, cotangent):
    shape = jax.ShapeDtypeStruct
    return pl.pallas_call(
        expert_kernel,
        out_shape=(
            shape((TOK, WIDTH), BF16),
            shape((TOK, WIDTH), F32),
            shape((TOK, WIDTH), BF16),
            shape((16, WIDTH), F32),
            shape((512, 256), BF16),
            shape((WIDTH, FF), BF16),
            shape((FF, WIDTH), BF16),
        ),
        in_specs=[VMEM] * 6 + [ANY] * 2 + [VMEM],
        out_specs=(VMEM,) * 5 + (ANY,) * 2,
        scratch_shapes=[
            pltpu.VMEM((WIDTH, FF), BF16),
            pltpu.VMEM((FF, WIDTH), BF16),
            pltpu.VMEM((TOK, WIDTH), F32),
            pltpu.VMEM((2 * TOK, 16 * CAP), BF16),
            pltpu.VMEM((16 * CAP, WIDTH), BF16),
            pltpu.VMEM((16 * CAP, WIDTH), BF16),
            pltpu.VMEM((16 * CAP, WIDTH), BF16),
            pltpu.VMEM((16 * CAP, WIDTH), BF16),
            pltpu.VMEM((8 * CAP, FF), BF16),
            pltpu.VMEM((8 * CAP, FF), BF16),
            pltpu.VMEM((8 * CAP, WIDTH), BF16),
            pltpu.VMEM((8 * CAP, WIDTH), BF16),
            pltpu.VMEM((8 * CAP, WIDTH), F32),
            pltpu.VMEM((8 * CAP, WIDTH), F32),
            pltpu.VMEM((WIDTH, FF), BF16),
            pltpu.VMEM((FF, WIDTH), BF16),
            pltpu.VMEM((4, TOK, 256), BF16),
            pltpu.SemaphoreType.DMA((4,)),
            pltpu.SemaphoreType.DMA((20,)),
            pltpu.SemaphoreType.DMA((20,)),
        ],
        compiler_params=pltpu.CompilerParams(
            collective_id=1, has_side_effects=True, vmem_limit_bytes=VMEM_LIMIT
        ),
    )(att, inputs, out_w, gain, router_w, routes, w_in, w_out, cotangent)


SEM = {
    "gm": 0, "core_in": 4, "core_out": 5, "x_in": 6, "y_in": 10, "y_out": 11, "x_out": 12, "core_kv": 16, "y_kv": 24,
    "x_q": 28, "x_kv": 32, "a_core": 36, "a_z": 36, "a_q": 40, "a_x": 44, "t_core": 48, "t_z": 48, "t_q": 52, "t_x": 56,
}


def backward_kernel(
    p_ref, q_ref, kv_ref, own_ref, inv_ref, da_ref, norm_ref, gmix_ref, small_ref, inp_ref, gain_ref, w_ref,
    gmid_ref, gwi_hbm, gwo_hbm,
    gin_ref, gwin_ref, gwout_ref, b_ref, a_out_ref, table_ref,
    qexp, doexp, drow, accb, ds, dq, dkv, core_kv, y_send, y_kv, fin_kv, fin_q, home_q, home_kv, gm_all,
    dproj, wide, a_low, a_core, a_mid, a_z, a_mid2, a_q, a_last, small, trow, tabs, t_got,
    own_in, own_out, got_in, got_out, x_in, mid_in, y_in, y_out, x_out, local, send, recv,
):
    me = Place()
    load_in = pltpu.make_async_copy(gwi_hbm.at[:, me.c], own_in, local.at[0])
    load_in.start()
    load_out = pltpu.make_async_copy(gwo_hbm.at[:, me.c], own_out, local.at[1])
    load_out.start()
    greet(
        [me.core_peer()]
        + [me.x_peer(k) for k in (1, 2, 3)]
        + [me.z_peer(k) for k in (1, 2, 3)]
        + [me.q_peer(k) for k in (1, 2, 3)]
    )
    started = []

    def go(src, dst, name, step, peer):
        copy = rcopy(src, dst, send, recv, SEM[name] + step, peer)
        copy.start()
        started.append(copy)
        return copy

    core_in = go(gwi_hbm.at[:, 1 - me.c], got_in, "core_in", 0, me.core_peer())
    core_out = go(gwo_hbm.at[:, 1 - me.c], got_out, "core_out", 0, me.core_peer())
    gm = [go(gmix_ref, gm_all.at[rows(me.x, TOK)], "gm", k, me.x_peer(k)) for k in (1, 3, 2)]
    gm_all[rows(me.x, TOK), :] = gmix_ref[...]

    lanes = iota((512, 256), 1)
    queries = q_ref[...].astype(F32) * SCALE
    da = da_ref[...].astype(F32)
    product = da * own_ref[...].astype(F32)
    sums = jnp.zeros((512, 128), F32)
    for h in range(3):
        inside = (lanes >= 64 * h) & (lanes < 64 * h + 64)
        qexp[pl.ds(512 * h, 512), :] = jnp.where(inside, queries, 0.0).astype(BF16)
        at = (128, 192, 64)[h]
        inside = (lanes >= at) & (lanes < at + 64)
        inv = inv_ref[:, pl.ds(h, 1)]
        doexp[pl.ds(512 * h, 512), :] = jnp.where(inside, da * inv, 0.0).astype(BF16)
        total = jnp.sum(jnp.where(inside, product, 0.0), axis=1, keepdims=True) * inv
        sums = jnp.where(iota((512, 128), 1) == h, total, sums)
    drow[...] = sums.T
    accb[...] = jnp.zeros_like(accb)
    dq[...] = jnp.zeros_like(dq)

    def core_copy(rel, xx, y):
        block = rows(4 * xx + 2 * y + 1 - me.c, TOK)
        return rcopy(
            dkv.at[block], core_kv.at[4 * rel + xx], send, recv, SEM["core_kv"] + 4 * rel + xx, me.core_peer()
        )

    def attend(rel, y):
        def one(xx, carry):
            span = rows(2 * xx + y, 256)
            keys = kv_ref[span, pl.ds(0, 256)]
            values = kv_ref[span, pl.ds(128, 256)]
            for h in range(3):
                cols = pl.ds(512 * h, 512)
                grads = dot_nt(values, doexp[cols, :])
                part = p_ref[span, cols].astype(F32) * (grads - drow[pl.ds(h, 1), :])
                ds[:, cols] = part.astype(BF16)
                for k in range(2):
                    for t in range(4):
                        kind = jnp.clip(4 * xx + 2 * y + k - (4 * t + 2 * me.y + me.c), -2, 2) + 2
                        accb[h, kind] += part[128 * k : 128 * k + 128, 128 * t : 128 * t + 128]
            dq[...] += dot_tn(keys, ds[...])
            gk = dot(ds[...], qexp[...])
            gv = dot(p_ref[span, :], doexp[...])
            dkv[span, pl.ds(0, 128)] = gk[:, :128].astype(BF16)
            dkv[span, pl.ds(128, 128)] = (gk[:, 128:] + gv[:, :128]).astype(BF16)
            dkv[span, pl.ds(256, 128)] = gv[:, 128:].astype(BF16)
            core_copy(rel, xx, y).start()
            return carry

        lax.fori_loop(0, 4, one, 0)

    attend(0, 1 - me.y)

    def to_y(xx):
        return rcopy(y_send.at[xx], y_kv.at[xx], send, recv, SEM["y_kv"] + xx, me.y_peer())

    def forward_y(xx, carry):
        core_copy(0, xx, 1 - me.y).wait_recv()
        own = dkv[rows(4 * xx + 2 * (1 - me.y) + me.c, TOK), :].astype(F32)
        y_send[xx] = (own + core_kv[xx].astype(F32)).astype(BF16)
        to_y(xx).start()
        return carry

    lax.fori_loop(0, 4, forward_y, 0)
    load_in.wait()
    core_in.wait_recv()

    def add_in(j, carry):
        own_in[j] = (own_in[j].astype(F32) + got_in[j].astype(F32)).astype(BF16)
        return carry

    lax.fori_loop(0, 8, add_in, 0)
    xs_in = [go(own_in.at[pl.ds(2 * me.x_of(k), 2)], x_in.at[k - 1], "x_in", k, me.x_peer(k)) for k in (1, 3, 2)]
    load_out.wait()
    core_out.wait_recv()

    def add_out(j, carry):
        own_out[j] = (own_out[j].astype(F32) + got_out[j].astype(F32)).astype(BF16)
        return carry

    lax.fori_loop(0, 8, add_out, 0)
    ys_out = []
    for xx in range(4):
        copy = rcopy(
            own_out.at[2 * xx + 1 - me.y], y_out.at[xx], send, recv, SEM_Y_OUT + xx, me.y_peer()
        )
        copy.start()
        started.append(copy)
        ys_out.append(copy)

    attend(1, me.y)

    fin_q_t = jnp.concatenate(
        [
            dq[pl.ds(0, 64), pl.ds(0, 512)],
            dq[pl.ds(64, 64), pl.ds(512, 512)],
            dq[pl.ds(128, 64), pl.ds(1024, 512)],
            jnp.zeros((64, 512), F32),
        ],
        axis=0,
    )
    fin_q[...] = (fin_q_t * SCALE).T.astype(BF16)
    xs_q = [
        go(fin_q.at[rows(me.x_of(k), TOK)], home_q.at[me.x], "x_q", k, me.x_peer(k)) for k in (1, 3, 2)
    ]
    home_q[me.x] = fin_q[rows(me.x, TOK), :]
    xs_kv = []
    for k in (1, 3, 2, 0):
        xx = me.x_of(k)
        core_copy(1, xx, me.y).wait_recv()
        to_y(xx).wait_recv()
        own = dkv[rows(4 * xx + 2 * me.y + me.c, TOK), :].astype(F32)
        block = (own + core_kv[4 + xx].astype(F32) + y_kv[xx].astype(F32)).astype(BF16)
        fin_kv[rows(xx, TOK), :] = block
        if k:
            xs_kv.append(go(fin_kv.at[rows(xx, TOK)], home_kv.at[me.x], "x_kv", k, me.x_peer(k)))
        else:
            home_kv[me.x] = block

    tile = iota((128, 128), 0) - iota((128, 128), 1)
    before, middle, after = bucket_tile(tile - 128), bucket_tile(tile), bucket_tile(tile + 128)

    def bucket_sum(b, carry):
        for h in range(3):
            near = (
                jnp.where(before == b, accb[h, 1], 0.0)
                + jnp.where(middle == b, accb[h, 2], 0.0)
                + jnp.where(after == b, accb[h, 3], 0.0)
            )
            trow[h, pl.ds(b, 1), :] = jnp.sum(near, axis=0, keepdims=True)
        return carry

    lax.fori_loop(0, BUCKETS, bucket_sum, 0)
    table = jnp.zeros((BUCKETS, 128), F32)
    for h in range(3):
        trow[h, pl.ds(BUCKETS // 2 - 1, 1), :] += jnp.sum(accb[h, 0], axis=0, keepdims=True)
        trow[h, pl.ds(BUCKETS - 1, 1), :] += jnp.sum(accb[h, 4], axis=0, keepdims=True)
        total = jnp.sum(trow[h], axis=1, keepdims=True)
        table = jnp.where(iota((BUCKETS, 128), 1) == 3 * me.x + h, total, table)
    tabs[0] = table
    t_core = go(tabs.at[0], t_got.at[0], "t_core", 0, me.core_peer())

    wide[:, pl.ds(0, 256)] = dot_tn(norm_ref[...], fin_q[...])
    wide[:, pl.ds(256, 384)] = dot_tn(norm_ref[...], fin_kv[...])
    for copy in gm:
        copy.wait_recv()
    att_wide = dot(own_ref[...], out_places()).astype(BF16)
    from_out = dot_tn(att_wide, gm_all[...])
    wide[:, pl.ds(0, 640)] += from_out[:, :640]
    wide[:, pl.ds(640, 128)] = from_out[:, 640:]

    t_core.wait_recv()
    tabs[1] = tabs[0] + t_got[0]
    ts = [go(tabs.at[1], t_got.at[k], "t_z", k, me.z_peer(k)) for k in (1, 3, 2)]
    for copy in xs_q + xs_kv:
        copy.wait_recv()

    def piece(p, j):
        g, t = j // 3, j % 3
        if p == 0:
            return home_q[g, :, pl.ds(128 * (t // 2), 128)].astype(F32), t % 2
        if p == 1:
            return home_kv[g, :, pl.ds(128 * (t // 2), 128)].astype(F32), t % 2
        at, half = ((2, 0), (2, 1), (1, 1))[t]
        return home_kv[g, :, pl.ds(128 * at, 128)].astype(F32), half

    for p in range(3):
        for n in range(6):
            first, half_first = piece(p, 2 * n)
            second, half_second = piece(p, 2 * n + 1)
            dproj[p, :, pl.ds(128 * n, 128)] = pair(first, half_first, second, half_second).astype(BF16)
    gnorm = dot_nt(dproj[0], w_ref[0]) + dot_nt(dproj[1], w_ref[1]) + dot_nt(dproj[2], w_ref[2])
    inputs = inp_ref[...].astype(F32)
    root = lax.rsqrt(jnp.mean(inputs * inputs, axis=1, keepdims=True) + EPSILON)
    small[...] = jnp.zeros_like(small)
    small[pl.ds(0, 16), :] = small_ref[...]
    small[pl.ds(0, 1), :] = jnp.sum(gnorm * inputs * root, axis=0, keepdims=True)
    u = gain_ref[...] * gnorm
    mean = jnp.mean(u * inputs, axis=1, keepdims=True)
    gin_ref[...] = gmid_ref[...] + root * u - inputs * (root * root * root * mean)
    wide[:, pl.ds(640, 128)] += dot(small[...].astype(BF16), norm_places()).T
    a_low[...] = wide[...].astype(BF16)
    ac = go(a_low.at[rows(1 - me.c, 512)], a_core, "a_core", 0, me.core_peer())

    for copy in xs_in:
        copy.wait_recv()
    for j in range(2):
        total = own_in[2 * me.x + j].astype(F32)
        for k in range(3):
            total = total + x_in[k, j].astype(F32)
        mid_in[j] = total.astype(BF16)
    ys_in = go(mid_in.at[1 - me.y], y_in, "y_in", 0, me.y_peer())

    ac.wait_recv()
    a_mid[...] = (a_low[rows(me.c, 512), :].astype(F32) + a_core[...].astype(F32)).astype(BF16)
    az = [go(a_mid.at[rows(me.z_of(k), 128)], a_z.at[k - 1], "a_z", k, me.z_peer(k)) for k in (1, 3, 2)]

    for copy in ys_out:
        copy.wait_recv()
    for xx in range(4):
        y_out[xx] = (own_out[2 * xx + me.y].astype(F32) + y_out[xx].astype(F32)).astype(BF16)
    xs_out = [go(y_out.at[me.x_of(k)], x_out.at[k - 1], "x_out", k, me.x_peer(k)) for k in (1, 3, 2)]

    for copy in ts:
        copy.wait_recv()
    tabs[2] = tabs[1] + t_got[1] + t_got[2] + t_got[3]
    ts = [go(tabs.at[2], t_got.at[3 + k], "t_q", k, me.q_peer(k)) for k in (1, 3, 2)]
    for copy in az:
        copy.wait_recv()
    total = a_mid[rows(me.z, 128), :].astype(F32)
    for k in range(3):
        total = total + a_z[k].astype(F32)
    a_mid2[...] = total.astype(BF16)
    aq = [go(a_mid2.at[rows(me.q_of(k), 32)], a_q.at[k - 1], "a_q", k, me.q_peer(k)) for k in (1, 3, 2)]

    for copy in ts:
        copy.wait_recv()
    tabs[3] = tabs[2] + t_got[4] + t_got[5] + t_got[6]
    ts = [go(tabs.at[3], t_got.at[6 + k], "t_x", k, me.x_peer(k)) for k in (1, 3, 2)]
    for copy in aq:
        copy.wait_recv()
    total = a_mid2[rows(me.q, 32), :].astype(F32)
    for k in range(3):
        total = total + a_q[k].astype(F32)
    a_last[...] = total
    a_out_ref[...] = total
    ax = [go(a_last.at[rows(me.x_of(k), 8)], b_ref.at[me.x], "a_x", k, me.x_peer(k)) for k in (1, 3, 2)]
    b_ref[me.x] = a_last[rows(me.x, 8), :]

    ys_in.wait_recv()
    gwin_ref[...] = mid_in[me.y].astype(F32) + y_in[...].astype(F32)
    for copy in xs_out:
        copy.wait_recv()
    total = y_out[me.x].astype(F32)
    for k in range(3):
        total = total + x_out[k].astype(F32)
    gwout_ref[...] = total
    for copy in ts:
        copy.wait_recv()
    table_ref[...] = tabs[3] + t_got[7] + t_got[8] + t_got[9]
    for copy in ax:
        copy.wait_recv()
    for copy in started:
        copy.wait_send()
    for rel, y in ((0, 1 - me.y), (1, me.y)):
        for xx in range(4):
            core_copy(rel, xx, y).wait_send()
    for xx in range(4):
        to_y(xx).wait_send()


SEM_Y_OUT = 60
SEMS = 64


def backward(p, q, kv, own, inv, da, norm, gmix, small, inputs, gain, w, gmid, gwi, gwo):
    shape = jax.ShapeDtypeStruct
    return pl.pallas_call(
        backward_kernel,
        out_shape=(
            shape((TOK, WIDTH), F32),
            shape((48, FF), F32),
            shape((192, WIDTH), F32),
            shape((4, 8, WIDTH), F32),
            shape((32, WIDTH), F32),
            shape((BUCKETS, 128), F32),
        ),
        in_specs=[VMEM] * 13 + [ANY] * 2,
        out_specs=(VMEM,) * 6,
        scratch_shapes=[
            pltpu.VMEM((1536, 256), BF16),
            pltpu.VMEM((1536, 256), BF16),
            pltpu.VMEM((128, 512), F32),
            pltpu.VMEM((3, 5, 128, 128), F32),
            pltpu.VMEM((256, 1536), BF16),
            pltpu.VMEM((256, 1536), F32),
            pltpu.VMEM((2048, 384), BF16),
            pltpu.VMEM((8, TOK, 384), BF16),
            pltpu.VMEM((4, TOK, 384), BF16),
            pltpu.VMEM((4, TOK, 384), BF16),
            pltpu.VMEM((512, 384), BF16),
            pltpu.VMEM((512, 256), BF16),
            pltpu.VMEM((4, TOK, 256), BF16),
            pltpu.VMEM((4, TOK, 384), BF16),
            pltpu.VMEM((512, WIDTH), BF16),
            pltpu.VMEM((3, TOK, WIDTH), BF16),
            pltpu.VMEM((1024, WIDTH), F32),
            pltpu.VMEM((1024, WIDTH), BF16),
            pltpu.VMEM((512, WIDTH), BF16),
            pltpu.VMEM((512, WIDTH), BF16),
            pltpu.VMEM((3, 128, WIDTH), BF16),
            pltpu.VMEM((128, WIDTH), BF16),
            pltpu.VMEM((3, 32, WIDTH), BF16),
            pltpu.VMEM((32, WIDTH), F32),
            pltpu.VMEM((128, WIDTH), F32),
            pltpu.VMEM((3, BUCKETS, 128), F32),
            pltpu.VMEM((4, BUCKETS, 128), F32),
            pltpu.VMEM((10, BUCKETS, 128), F32),
            pltpu.VMEM((8, 48, FF), BF16),
            pltpu.VMEM((8, 192, WIDTH), BF16),
            pltpu.VMEM((8, 48, FF), BF16),
            pltpu.VMEM((8, 192, WIDTH), BF16),
            pltpu.VMEM((3, 2, 48, FF), BF16),
            pltpu.VMEM((2, 48, FF), BF16),
            pltpu.VMEM((48, FF), BF16),
            pltpu.VMEM((4, 192, WIDTH), BF16),
            pltpu.VMEM((3, 192, WIDTH), BF16),
            pltpu.SemaphoreType.DMA((2,)),
            pltpu.SemaphoreType.DMA((SEMS,)),
            pltpu.SemaphoreType.DMA((SEMS,)),
        ],
        compiler_params=pltpu.CompilerParams(
            collective_id=2, has_side_effects=True, vmem_limit_bytes=VMEM_LIMIT
        ),
    )(p, q, kv, own, inv, da, norm, gmix, small, inputs, gain, w, gmid, gwi, gwo)


def body(
    block_input, gain_one, qkv_weight, out_weight, rel_table, gain_two, router_weight, routes, w_in, w_out, cotangent
):
    inputs = block_input[0]
    att, own, q, kv, p, inv, norm = forward(inputs, gain_one[None], qkv_weight, rel_table)
    y, gmid, gmix, small, da, gwi, gwo = expert(
        att, inputs, out_weight, gain_two[None], router_weight, routes[0], w_in, w_out, cotangent[0]
    )
    gin, gwin, gwout, b, a, table = backward(
        p, q, kv, own, inv, da, norm, gmix, small, inputs, gain_one[None], qkv_weight, gmid,
        gwi.reshape(8, 2, 48, FF), gwo.reshape(8, 2, 192, WIDTH),
    )
    b = b[:, :6]

    def columns(*spans):
        part = jnp.concatenate([b[:, :, s : s + n] for s, n in spans], axis=2)
        return jnp.transpose(part, (1, 0, 2)).reshape(6, WIDTH)

    grad_qkv = jnp.stack([columns((0, 192)), columns((256, 192)), columns((512, 128), (448, 64))])
    grad_out = a.reshape(4, 8, WIDTH)[:3, 6:].reshape(6, WIDTH)
    total = jnp.sum(b[:, :, 640:], axis=0)
    return (
        y[None],
        gin[None],
        total[:, 0],
        grad_qkv,
        grad_out,
        table[:, :HEADS],
        total[:, 1],
        total[:, 8:16],
        gwin[None],
        gwout[None],
    )


def solution(mesh):
    tokens = P("expert", "ctx", None)
    split = P(("ctx", "expert"))
    return jax.shard_map(
        body,
        mesh=mesh,
        in_specs=(
            tokens, P(), P(), P(), P(), P(), P(), tokens, P("expert", None, None), P("expert", None, None), tokens,
        ),
        out_specs=(
            tokens, tokens, split, P(None, ("ctx", "expert"), None), split, P(), split, split, tokens, tokens,
        ),
        check_vma=False,
    )
```

time: 1690 us -> 180 us (0.11)
  starting transfers between devices: 425 us -> 0 us
  blocking collectives: 416 us -> 0 us
  local copies, waits for them, and re-layouts: 291 us -> 19.2 us
  other arithmetic: 254 us -> 1.4 us
  matrix products: 182 us -> 0 us
  Pallas kernels: 0 us -> 157 us
  waiting for transfers between devices: 92.9 us -> 0 us
    unnamed x2 -> x0, blocking collectives: 416 us -> none
    ppermute x64 -> x0, starting transfers between devices: 306 us -> none  [from_behind(): return lax.ppermute(value, axis, pairs)]
    dot_general x114 -> x0, matrix products: 182 us -> none  [the longest x16 32.7 us: block_grads(): jnp.einsum('hqk,khd->qhd', grad_raw, key_heads, preferred_element_type=jn...]
    pallas_call x0 -> x3, Pallas kernels: none -> 157 us  [the longest x1 78.1 us: backward(): pl.pallas_call(backward_kernel, out_shape=(shape((TOK, WIDTH), F32), shap...]
    unnamed x33 -> x0, starting transfers between devices: 99.4 us -> none
    convert_element_type x69 -> x0, other arithmetic: 83.8 us -> none  [the longest x32 54.3 us: turn(): part.astype(own.dtype)]
    while x303 -> x0, local copies, waits for them, and re-layouts: 75.3 us -> none
    add x99 -> x0, other arithmetic: 73.6 us -> none  [the longest x16 30.4 us: step_keys(): local[0] + grad_query]
  transfers between devices with their start and end apart: 105 -> 0, of which waited for: 7 -> 0; matrix products, arithmetic and copies ran while one was open for 52% -> 0% of each run, Pallas kernels for 0% -> 0%
where the time goes in v1:
time: 180 us; the launch traced here: 178 us
  Pallas kernels  157 us (87%)
  local copies, waits for them, and re-layouts  19.2 us (11%)
    pallas_call x1, Pallas kernels, backward(): pl.pallas_call(backward_kernel, out_shape=(shape((TOK, WIDTH), F32), shap...  78.1 us
    pallas_call x1, Pallas kernels, forward(): pl.pallas_call(forward_kernel, out_shape=(shape((4, TOK, 256), BF16), sha...  42.6 us
    pallas_call x1, Pallas kernels, expert(): pl.pallas_call(expert_kernel, out_shape=(shape((TOK, WIDTH), BF16), shape...  35.8 us
    unnamed x9, local copies, waits for them, and re-layouts  10.6 us

profile of v1, /device:TPU:1, one launch (start us, length us, event | category | flops | bytes accessed | tf_op | source)
XLA Modules:
  0.0 177.8 jit_solution(1860787282252537028)
XLA Ops:
  0.6 1.3 broadcast_in_dim.19.gain_ref
  1.9 1.4 copy.25.table_ref
  3.3 42.6 %shard_map.186 = (bf16[4,128,256]{2,1,0:T(8,128)(2,1)}, bf16[512,256]{1,0:T(8,128)(2,1)}, bf16[512,256]{1,0:T(8,128)(2,1)}, bf16[2048,384]{1,0:T(8,128)(2,1)}, b...) custom-call(bf16[128,768]{1,0:T(8,128)(2,1)} %bitcast.19, ...), custom_call_target="tpu_custom_call" | custom-call | tf_op jit(solution)/shard_map/pallas_call | solution.py:319
  45.9 1.3 broadcast_in_dim.20.gain_ref
  47.2 1.5 copy.26.router_ref
  48.7 1.4 copy.27.routes_ref
  50.1 35.8 %shard_map.187 = (bf16[128,768]{1,0:T(8,128)(2,1)}, f32[128,768]{1,0:T(8,128)}, bf16[128,768]{1,0:T(8,128)(2,1)}, f32[16,768]{1,0:T(8,128)}, bf16[512,256]{1,0:T...) custom-call(bf16[4,128,256]{2,1,0:T(8,128)(2,1)} %get-tuple-element.30.att_ref, ...), custom_call_target="tpu_custom_call" | custom-call | tf_op jit(solution)/shard_map/pallas_call | solution.py:488
  85.9 0.0 copy-start
  85.9 78.1 %shard_map.188 = (f32[128,768]{1,0:T(8,128)}, f32[48,3072]{1,0:T(8,128)}, f32[192,768]{1,0:T(8,128)}, f32[4,8,768]{2,1,0:T(8,128)}, f32[32,768]{1,0:T(8,128)}, /*index=5*/f32[32,128]{1,0:T(8,128)}) custom-call(bf16[2048,1536]{1,0:T(8,128)(2,1)} %get-tuple-element.32.p_ref, bf16[512,256]{1,0:T(8,128)(2,1)} %get-tuple-element.33.q_ref, ...), custom_call_target="tpu_custom_call" | custom-call | tf_op jit(solution)/shard_map/pallas_call | solution.py:822
  164.0 0.7 fusion
  164.8 0.7 slice_reduce_fusion.1
  165.5 0.8 slice.41
  166.3 0.1 stack_reshape.11
  166.4 0.8 slice_bitcast_fusion.1
  167.2 0.1 stack_reshape.10
  167.3 0.1 stack_reshape.9
  167.3 0.6 pad_maximum_fusion
  168.0 0.9 slice.46
  168.9 0.6 reshape.35
  169.5 1.4 copy.31
  170.9 0.7 slice.45
  171.6 0.0 copy-done
  171.6 0.7 copy.36
  172.2 1.8 copy.37
  174.0 1.9 %copy.38 = f32[1,48,3072]{2,1,0:T(8,128)} copy(f32[1,48,3072]{2,1,0:T(8,128)} %bitcast.23) | data formatting | bytes 1179648
  175.9 1.9 %copy.39 = f32[1,192,768]{2,1,0:T(8,128)} copy(f32[1,192,768]{2,1,0:T(8,128)} %bitcast.22) | data formatting | bytes 1179648
  (4 shorter events, 0.0 us)
Async XLA Ops:
  85.9 85.6 %copy-start = (bf16[128,768]{1,0:T(8,128)(2,1)S(1)}, bf16[128,768]{1,0:T(8,128)(2,1)}, u32[]{:S(2)}) copy-start(bf16[128,768]{1,0:T(8,128)(2,1)} %get-tuple-element.31) | copy-start | bytes 589828

commit v2 on v0

v2 whole, which is shorter than its diff:
```python
import jax
import jax.numpy as jnp
import numpy as np
from jax import lax
from jax.experimental import pallas as pl
from jax.experimental.pallas import tpu as pltpu
from jax.sharding import PartitionSpec as P

HEADS = 12
HEAD_DIM = 64
BUCKETS = 32
MAX_DISTANCE = 128
EPSILON = 1e-06
SCALE = HEAD_DIM ** (-0.5)
TOK = 128
WIDTH = 768
FF = 3072
CAP = 24
F32 = jnp.float32
BF16 = jnp.bfloat16
MESH = pl.DeviceIdType.MESH
VMEM = pl.BlockSpec(memory_space=pltpu.VMEM)
SMEM = pl.BlockSpec(memory_space=pltpu.SMEM)
ANY = pl.BlockSpec(memory_space=pl.ANY)
VMEM_LIMIT = 63 * 1024 * 1024


def bucket_edges(buckets, reach):
    half = buckets // 2
    exact = half // 2
    spans = np.arange(1, reach + 1)
    spread = np.log(np.maximum(spans, exact) / exact) / np.log(reach / exact) * (half - exact)
    large = np.minimum(exact + spread.astype(np.int64), half - 1)
    level = np.where(spans < exact, spans, large)
    return [int(np.argmax(level >= b)) + 1 for b in range(1, half)]


EDGES = bucket_edges(BUCKETS, MAX_DISTANCE)


def dot(a, b):
    return jnp.dot(a, b, preferred_element_type=F32)


def dot_nt(a, b):
    return lax.dot_general(a, b, (((1,), (1,)), ((), ())), preferred_element_type=F32)


def dot_tn(a, b):
    return lax.dot_general(a, b, (((0,), (0,)), ((), ())), preferred_element_type=F32)


def iota(shape, dim):
    return lax.broadcasted_iota(jnp.int32, shape, dim)


class Place:
    def __init__(self):
        self.i = lax.axis_index("ctx")
        self.e = lax.axis_index("expert")
        self.x = lax.div(self.i, 4)
        self.y = lax.rem(lax.div(self.i, 2), 2)
        self.c = lax.rem(self.i, 2)
        self.z = lax.div(self.e, 2)
        self.h = lax.rem(self.e, 2)
        self.q = self.h * 2 + self.y

    def x_of(self, step):
        return lax.rem(self.x + 4 + step, 4)

    def x_peer(self, step):
        return (4 * self.x_of(step) + 2 * self.y + self.c, self.e)

    def core_peer(self):
        return (4 * self.x + 2 * self.y + 1 - self.c, self.e)

    def y_peer(self):
        return (4 * self.x + 2 * (1 - self.y) + self.c, self.e)

    def z_of(self, step):
        return lax.rem(self.z + 4 + step, 4)

    def z_peer(self, step):
        return (self.i, 2 * self.z_of(step) + self.h)

    def q_of(self, step):
        return lax.rem(self.q + 4 + step, 4)

    def q_peer(self, step):
        q = self.q_of(step)
        return (4 * self.x + 2 * lax.rem(q, 2) + self.c, 2 * self.z + lax.div(q, 2))

    def corner_peer(self):
        return (4 * self.x + 2 * (1 - self.y) + self.c, 2 * self.z + 1 - self.h)

    def e_of(self, step):
        return lax.rem(self.e + 8 + step, 8)

    def e_peer(self, step):
        return (self.i, self.e_of(step))


def greet(peers):
    barrier = pltpu.get_barrier_semaphore()
    for peer in peers:
        pl.semaphore_signal(barrier, inc=1, device_id=peer, device_id_type=MESH)
    pl.semaphore_wait(barrier, len(peers))


def rcopy(src, dst, send, recv, slot, peer):
    return pltpu.make_async_remote_copy(
        src_ref=src,
        dst_ref=dst,
        send_sem=send.at[slot],
        recv_sem=recv.at[slot],
        device_id=peer,
        device_id_type=MESH,
    )


def rows(index, size):
    return pl.ds(pl.multiple_of(index * size, size), size)


def pair(first, half_first, second, half_second):
    if first is second and (half_first, half_second) == (0, 1):
        return first
    low = pltpu.roll(first, 64, 1) if half_first else first
    high = second if half_second else pltpu.roll(second, 64, 1)
    return jnp.where(iota(low.shape, 1) < 64, low, high)


def norm_places():
    col = iota((1, 1024), 1)
    r = col & 7
    xx = (col >> 3) & 3
    yl = (col >> 5) & 1
    e = (((col >> 7) & 3) << 1) + ((col >> 6) & 1)
    c = (col >> 9) & 1
    d = jnp.where(r < 6, 192 * xx + 96 * yl + 48 * c + 6 * e + r, -1)
    return (iota((WIDTH, 1024), 0) == d).astype(F32).astype(BF16)


def att_places(group):
    col = iota((1, 1024), 1)
    r = col & 7
    e = (((col >> 7) & 3) << 1) + ((col >> 6) & 1)
    f = 96 * ((col >> 5) & 1) + 48 * ((col >> 9) & 1) + 6 * e + r
    f = jnp.where((r < 6) & (((col >> 3) & 3) == group), f, -1)
    lane = iota((256, 1024), 0)
    feature = jnp.where(lane >= 128, lane - 128, jnp.where(lane >= 64, lane + 64, -2))
    return (feature == f).astype(F32).astype(BF16)


def bucket_tile(offset):
    length = jnp.abs(offset)
    level = jnp.where(offset > 0, BUCKETS // 2, 0)
    for edge in EDGES:
        level = level + (length >= edge).astype(jnp.int32)
    return level


SEMS = 192


class Mail:
    def __init__(self, send, recv):
        self.send, self.recv, self.used, self.started = send, recv, 0, []

    def block(self, count):
        base = self.used
        self.used += count
        assert self.used <= SEMS
        return base

    def copy(self, src, dst, slot, peer):
        return rcopy(src, dst, self.send, self.recv, slot, peer)

    def go(self, src, dst, slot, peer):
        copy = self.copy(src, dst, slot, peer)
        copy.start()
        self.started.append(copy)
        return copy

    def sent(self, copy):
        copy.wait_send()
        self.started = [other for other in self.started if other is not copy]

    def go_later(self, make):
        copy = Made(lambda: self.copy(*make()))
        copy.make().start()
        self.started.append(copy)
        return copy


class Made:
    def __init__(self, make):
        self.make = make

    def wait_recv(self):
        self.make().wait_recv()

    def wait_send(self):
        self.make().wait_send()


def wait_all(copies):
    for copy in copies:
        copy.wait_recv()


def layer_kernel(
    inp_ref, gain1_ref, w_ref, table_ref, out_w_ref, gain2_ref, router_ref, routes_ref, w_in_hbm, w_out_hbm, cot_ref,
    y_ref, gin_ref, gwin_ref, gwout_ref, gqkv_ref, gout_ref, gain_ref, gtable_ref,
    norm_all, norm_own, q_all, kv, qexp, p_ref, scale, own, att,
    middle, select, rows_out, rows_got, back_got, gwi, gwo, gmid, gmix, da_send, da,
    core_kv, y_kv, home_q, home_kv, small,
    o_core, o_z, o_mid2, o_q, o_last, o_x,
    q_core, q_z, q_mid2, q_q, q_last, q_x,
    k_core, k_z, k_mid2, k_q, k_last, k_x,
    trow, tabs, t_got, got_in, got_out, x_far, x_near, y_in, y_out, z_far, z_near,
    local, send, recv,
):
    me = Place()
    mail = Mail(send, recv)
    near = [1, 3, 2]
    others = [1, 7, 2, 6, 3, 5, 4]
    barrier = pltpu.get_barrier_semaphore()
    peers = [me.x_peer(k) for k in near] + [me.core_peer(), me.y_peer(), me.corner_peer()]
    peers = peers + [me.e_peer(k) for k in others]
    for peer in peers:
        pl.semaphore_signal(barrier, inc=1, device_id=peer, device_id_type=MESH)

    inputs = inp_ref[...].astype(F32)
    root1 = lax.rsqrt(jnp.mean(inputs * inputs, axis=1, keepdims=True) + EPSILON)
    normed = (inputs * root1 * gain1_ref[...].reshape(1, WIDTH)).astype(BF16)
    proj = [dot(normed, w_ref[p]) for p in range(3)]

    def join(p, a, s, b):
        first = proj[p][:, 128 * (a // 2) : 128 * (a // 2) + 128]
        second = first if (p == s and a // 2 == b // 2) else proj[s][:, 128 * (b // 2) : 128 * (b // 2) + 128]
        return pair(first, a % 2, second, b % 2)

    block = rows(me.i, TOK)
    mine = rows(me.x, TOK)
    s_kv, s_q, s_y, s_c, s_f = [mail.block(4) for _ in range(5)]
    def source(step, y, c):
        return rows(4 * me.x_of(-step) + 2 * y + c, TOK)

    ys, cs = {}, {}

    def pass_on(step):
        def to(slot, peer):
            part = kv.at[source(step, me.y, me.c)]
            return part, part, slot + step, peer()

        ys[step] = mail.go_later(lambda: to(s_y, me.y_peer))
        cs[step] = mail.go_later(lambda: to(s_c, me.core_peer))

    tile = iota((128, 128), 0) - iota((128, 128), 1)
    lanes = iota((512, 256), 1)
    def attention(s_ref, bias, m_ref, l_ref, acc, o_part, o_t, kv_send, q_send):
        for g in range(4):
            a = 3 * g
            kv_send[g, :, pl.ds(0, 128)] = join(1, a, 1, a + 1).astype(BF16)
            kv_send[g, :, pl.ds(128, 128)] = join(1, a + 2, 2, a + 2).astype(BF16)
            kv_send[g, :, pl.ds(256, 128)] = join(2, a, 2, a + 1).astype(BF16)
            q_send[g, :, pl.ds(0, 128)] = join(0, a, 0, a + 1).astype(BF16)
            q_send[g, :, pl.ds(128, 128)] = jnp.where(iota((TOK, 128), 1) < 64, join(0, a + 2, 0, a + 2), 0.0).astype(BF16)
        pl.semaphore_wait(barrier, len(peers))
        kvs = {k: mail.go(kv_send.at[me.x_of(k)], kv.at[block], s_kv + k, me.x_peer(k)) for k in near}
        kv[block, :] = kv_send[me.x]
        qs = {k: mail.go(q_send.at[me.x_of(k)], q_all.at[mine], s_q + k, me.x_peer(k)) for k in near}
        q_all[mine, :] = q_send[me.x]

        pass_on(0)
        norm_own[...] = dot(normed, norm_places()).astype(BF16)
        norm_all[mine, :] = norm_own[...]
        for h in range(3):
            head = 3 * me.x + h

            def chain(first, n):
                value = jnp.full((128, 128), 1.0, F32) * table_ref[head, first]
                for level, edge in enumerate(EDGES):
                    value = jnp.where(n >= edge, table_ref[head, first + level + 1], value)
                return value

            bias[h, 0] = jnp.full((128, 128), 1.0, F32) * table_ref[head, BUCKETS // 2 - 1]
            bias[h, 1] = chain(0, 128 - tile)
            bias[h, 2] = jnp.where(tile > 0, chain(BUCKETS // 2, tile), chain(0, -tile))
            bias[h, 3] = chain(BUCKETS // 2, 128 + tile)
            bias[h, 4] = jnp.full((128, 128), 1.0, F32) * table_ref[head, BUCKETS - 1]
        m_ref[...] = jnp.full(m_ref.shape, -jnp.inf, F32)
        l_ref[...] = jnp.zeros(l_ref.shape, F32)
        wait_all(qs.values())
        queries = q_all[...].astype(F32) * SCALE
        for h in range(3):
            inside = (lanes >= 64 * h) & (lanes < 64 * h + 64)
            qexp[pl.ds(512 * h, 512), :] = jnp.where(inside, queries, 0.0).astype(BF16)

        def score(first, last, half, y, c):
            def one(step, carry):
                xx = me.x_of(-step)
                b = 4 * xx + 2 * y + c
                keys = kv[rows(b, TOK), pl.ds(0, 256)]
                for h in range(3):
                    s = dot_nt(keys, qexp[pl.ds(512 * h, 512), :])
                    for t in range(4):
                        kind = jnp.clip(b - (4 * t + 2 * me.y + me.c), -2, 2) + 2
                        part = s[:, 128 * t : 128 * t + 128] + bias[h, kind]
                        cols = pl.ds(128 * t, 128)
                        s_ref[h, rows(2 * xx + c, TOK), cols] = part
                        m_ref[half, h, :, cols] = jnp.maximum(
                            m_ref[half, h, :, cols], jnp.max(part.reshape(16, 8, 128), axis=0)
                        )
                return carry

            lax.fori_loop(first, last, one, 0)

        def weigh(half, y):
            for h in range(3):
                top = jnp.max(m_ref[half, h], axis=0, keepdims=True)
                acc[...] = jnp.zeros(acc.shape, F32)

                def one(xx, carry):
                    part = jnp.exp(s_ref[h, rows(xx, 256), :] - top)
                    l_ref[half, h] += jnp.sum(part.reshape(32, 8, 512), axis=0)
                    low = part.astype(BF16)
                    span = rows(2 * xx + y, 256)
                    p_ref[span, pl.ds(512 * h, 512)] = low
                    acc[...] += dot_tn(kv[span, pl.ds(128, 256)], low)
                    return carry

                lax.fori_loop(0, 4, one, 0)
                at = pl.ds((128, 192, 64)[h], 64)
                o_part[half, at, :] = acc[at, :]

        score(0, 1, 0, me.y, me.c)
        for k in near:
            kvs[k].wait_recv()
            pass_on(k)
        score(1, 4, 0, me.y, me.c)
        for k in range(4):
            cs[k].wait_recv()
        score(0, 4, 0, me.y, 1 - me.c)
        fs = {}
        for k in (0, 1, 3, 2):
            ys[k].wait_recv()

            def to(k=k):
                part = kv.at[source(k, 1 - me.y, me.c)]
                return part, part, s_f + k, me.core_peer()

            fs[k] = mail.go_later(to)
        weigh(0, me.y)
        score(0, 4, 1, 1 - me.y, me.c)
        wait_all(fs.values())
        score(0, 4, 1, 1 - me.y, 1 - me.c)
        weigh(1, 1 - me.y)

        factors = jnp.zeros((128, 512), F32)
        which = iota((128, 512), 0)
        o_t[...] = jnp.zeros(o_t.shape, F32)
        for h in range(3):
            tops = [jnp.max(m_ref[half, h], axis=0, keepdims=True) for half in range(2)]
            top = jnp.maximum(tops[0], tops[1])
            fade = [jnp.exp(t - top) for t in tops]
            sums = [jnp.sum(l_ref[half, h], axis=0, keepdims=True) for half in range(2)]
            inv = 1.0 / (sums[0] * fade[0] + sums[1] * fade[1])
            fade = [f * inv for f in fade]
            at = pl.ds((128, 192, 64)[h], 64)
            o_t[at, :] = o_part[0, at, :] * fade[0] + o_part[1, at, :] * fade[1]
            for half in range(2):
                factors = jnp.where(which == 3 * half + h, fade[half], factors)
        scale[...] = factors.T
        own[...] = o_t[...].T.astype(BF16)
        for copy in list(kvs.values()) + list(qs.values()):
            mail.sent(copy)

    pl.run_scoped(
        attention,
        pltpu.VMEM((3, 1024, 512), F32),
        pltpu.VMEM((3, 5, 128, 128), F32),
        pltpu.VMEM((2, 3, 8, 512), F32),
        pltpu.VMEM((2, 3, 8, 512), F32),
        pltpu.VMEM((256, 512), F32),
        pltpu.VMEM((2, 256, 512), F32),
        pltpu.VMEM((256, 512), F32),
        pltpu.VMEM((4, TOK, 384), BF16),
        pltpu.VMEM((4, TOK, 256), BF16),
    )
    s_o, s_n = mail.block(4), mail.block(4)
    os = [mail.go(own.at[rows(me.x_of(k), TOK)], att.at[me.x], s_o + k, me.x_peer(k)) for k in near]
    ns = [mail.go(norm_own, norm_all.at[mine], s_n + k, me.x_peer(k)) for k in near]
    att[me.x] = own[mine, :]

    s_there, s_home = mail.block(8), mail.block(8)
    gain2 = gain2_ref[...].reshape(1, WIDTH)
    slots = rows(me.e, 2 * CAP)
    keep = {}

    def experts(hidden, ginner, made, garr, arrived, gprod):
        load_in = pltpu.make_async_copy(w_in_hbm, gwi, local.at[0])
        load_in.start()
        load_out = pltpu.make_async_copy(w_out_hbm, gwo, local.at[1])
        load_out.start()
        wait_all(os)
        mixed = inputs
        for g in range(4):
            mixed = mixed + dot(att[g, :, pl.ds(0, 128)], out_w_ref[pl.ds(192 * g + 64, 128), :])
            mixed = mixed + dot(att[g, :, pl.ds(128, 128)], out_w_ref[pl.ds(192 * g, 128), :])
        middle[...] = mixed
        root = lax.rsqrt(jnp.mean(mixed * mixed, axis=1, keepdims=True) + EPSILON)
        normed_two = (mixed * root * gain2).astype(BF16)
        logits = dot_nt(normed_two, router_ref[...])
        shifted = jnp.exp(logits - jnp.max(logits, axis=1, keepdims=True))
        router = shifted / jnp.sum(shifted, axis=1, keepdims=True)
        diagonal = iota((TOK, TOK), 0) == iota((TOK, TOK), 1)
        named = jnp.sum(jnp.where(diagonal, routes_ref[...].astype(F32), 0.0), axis=1, keepdims=True).astype(jnp.int32)
        chosen = (named == iota((TOK, 8), 1)).astype(F32)
        gate = jnp.sum(chosen * router, axis=1, keepdims=True)
        earlier = (iota((TOK, TOK), 0) > iota((TOK, TOK), 1)).astype(F32).astype(BF16)
        ranks = dot(earlier, chosen.astype(BF16))
        slot = jnp.sum(chosen * ranks, axis=1, keepdims=True).astype(jnp.int32)
        target = named * (2 * CAP) + slot
        column = iota((TOK, 16 * CAP), 1)
        select[pl.ds(0, TOK), :] = (column == target).astype(F32).astype(BF16)
        select[pl.ds(TOK, TOK), :] = (column == target + CAP).astype(F32).astype(BF16)
        dy = cot_ref[...].astype(F32)
        both = jnp.concatenate([normed_two, (gate * dy).astype(BF16)], axis=0)
        rows_out[...] = dot_tn(select[...], both).astype(BF16)
        there = [
            mail.go_later(
                lambda k=k: (rows_out.at[rows(me.e_of(k), 2 * CAP)], rows_got.at[slots], s_there + k, me.e_peer(k))
            )
            for k in others
        ]
        rows_got[slots, :] = rows_out[slots, :]
        made[...] = jnp.zeros(made.shape, F32)
        garr[...] = jnp.zeros(garr.shape, F32)
        load_in.wait()
        load_out.wait()
        wait_all(there)
        got = rows_got[...].astype(F32).reshape(8, 2 * CAP, WIDTH)
        arrived[...] = got[:, :CAP].reshape(8 * CAP, WIDTH).astype(BF16)
        gprod[...] = got[:, CAP:].reshape(8 * CAP, WIDTH).astype(BF16)
        chunk = 768

        def through(j, carry):
            cols = rows(j, chunk)
            for k in range(3):
                part = rows(3 * j + k, 256)
                inner = dot(arrived[...], gwi[:, :, :, part].reshape(WIDTH, 256))
                square = inner * inner
                slope = np.float32(np.sqrt(2 / np.pi))
                t = jnp.tanh(slope * inner * (1.0 + 0.044715 * square))
                half = 0.5 * (1.0 + t)
                hidden[:, part] = (inner * half).astype(BF16)
                w_out = gwo[pl.ds(2 * j, 2)].reshape(chunk, WIDTH)[256 * k : 256 * k + 256]
                back = dot_nt(gprod[...], w_out)
                lean = half + 0.5 * inner * (1.0 - t * t) * slope * (1.0 + 3 * 0.044715 * square)
                ginner[:, part] = (lean * back).astype(BF16)
            made[...] += dot(hidden[:, cols], gwo[pl.ds(2 * j, 2)].reshape(chunk, WIDTH))
            garr[...] += dot_nt(ginner[:, cols], gwi[:, :, :, cols].reshape(WIDTH, chunk))
            return carry

        lax.fori_loop(0, FF // chunk, through, 0)
        back = jnp.concatenate([made[...].reshape(8, CAP, WIDTH), garr[...].reshape(8, CAP, WIDTH)], axis=1)
        for copy in there:
            mail.sent(copy)
        rows_out[...] = back.reshape(16 * CAP, WIDTH).astype(BF16)
        keep["home"] = [
            mail.go_later(
                lambda k=k: (rows_out.at[rows(me.e_of(k), 2 * CAP)], back_got.at[slots], s_home + k, me.e_peer(k))
            )
            for k in others
        ]
        back_got[slots, :] = rows_out[slots, :]

        def grads_in(j, carry):
            cols = rows(j, 256)
            gwi[:, :, :, cols] = dot_tn(arrived[...], ginner[:, cols]).astype(BF16).reshape(8, 2, 48, 256)
            return carry

        lax.fori_loop(0, FF // 256, grads_in, 0)
        s_in = mail.block(1)
        keep["core_in"] = mail.go_later(lambda: (gwi.at[:, 1 - me.c], got_in, s_in, me.core_peer()))

        def grads_out(j, carry):
            gwo[j] = dot_tn(hidden[:, rows(j, 384)], gprod[...]).astype(BF16).reshape(2, 192, WIDTH)
            return carry

        lax.fori_loop(0, 8, grads_out, 0)
        s_out = mail.block(1)
        keep["core_out"] = mail.go_later(lambda: (gwo.at[:, 1 - me.c], got_out, s_out, me.core_peer()))
        return gate, chosen, router, root, normed_two

    gate, chosen, router, root, normed_two = pl.run_scoped(
        experts,
        pltpu.VMEM((8 * CAP, FF), BF16),
        pltpu.VMEM((8 * CAP, FF), BF16),
        pltpu.VMEM((8 * CAP, WIDTH), F32),
        pltpu.VMEM((8 * CAP, WIDTH), F32),
        pltpu.VMEM((8 * CAP, WIDTH), BF16),
        pltpu.VMEM((8 * CAP, WIDTH), BF16),
    )

    keep["core_in"].wait_recv()

    def add_in(j, carry):
        gwi[j, me.c] = (gwi[j, me.c].astype(F32) + got_in[j].astype(F32)).astype(BF16)
        return carry

    lax.fori_loop(0, 8, add_in, 0)
    s_far, s_ring = mail.block(2), mail.block(4)
    right, left = me.x_of(1), me.x_of(3)
    far = me.x_of(2)
    fars = [
        mail.go(gwi.at[2 * far, me.c], x_far.at[0], s_far, me.x_peer(1)),
        mail.go(gwi.at[2 * far + 1, me.c], x_far.at[1], s_far + 1, me.x_peer(3)),
    ]
    ring = [
        mail.go(gwi.at[2 * right + 1, me.c], x_near.at[1], s_ring, me.x_peer(1)),
        mail.go(gwi.at[2 * left, me.c], x_near.at[2], s_ring + 1, me.x_peer(3)),
    ]

    wait_all(keep["home"])
    returned = dot(select[pl.ds(0, TOK), :], back_got[...])
    gnorm = dot(select[pl.ds(TOK, TOK), :], back_got[...])
    mid = middle[...]
    dy = cot_ref[...].astype(F32)
    y_ref[...] = (mid + gate * returned).astype(BF16)
    ggate = jnp.sum(dy * returned, axis=1, keepdims=True)
    glogits = ggate * gate * (chosen - router)
    high = glogits.astype(BF16)
    rest = (glogits - high.astype(F32)).astype(BF16)
    gnorm = gnorm + dot(high, router_ref[...]) + dot(rest, router_ref[...])
    small[...] = jnp.zeros(small.shape, F32)
    small[pl.ds(8, 8), :] = dot_tn(high, normed_two) + dot_tn(rest, normed_two)
    small[pl.ds(0, 1), :] = jnp.sum(gnorm * mid * root, axis=0, keepdims=True)
    u = gain2 * gnorm
    gmiddle = dy + root * u - mid * (root * root * root * jnp.mean(u * mid, axis=1, keepdims=True))
    gmid[...] = gmiddle
    gmix[...] = gmiddle.astype(BF16)
    upper = iota((TOK, 128), 1) >= 64
    for g in range(4):
        front = dot_nt(gmix[...], out_w_ref[pl.ds(192 * g + 64, 128), :])
        da_send[g, :, pl.ds(0, 128)] = jnp.where(upper, front, 0.0).astype(BF16)
        da_send[g, :, pl.ds(128, 128)] = dot_nt(gmix[...], out_w_ref[pl.ds(192 * g, 128), :]).astype(BF16)
    s_da = mail.block(4)
    das = [mail.go(da_send.at[me.x_of(k)], da.at[mine], s_da + k, me.x_peer(k)) for k in near]
    da[mine, :] = da_send[me.x]

    def rest(doexp, drow, accb, ds, dq, dkv, y_send, fin_kv, fin_q, dproj, o_low, q_low, k_low):
        att_wide = dot(att[0], att_places(0))
        for g in range(1, 4):
            att_wide = att_wide + dot(att[g], att_places(g))
        att_wide = att_wide.astype(BF16)
        for part in range(4):
            block_rows = dot_tn(att_wide[:, 256 * part : 256 * part + 256], gmix[...]).astype(BF16)
            o_low[part // 2, pl.ds(2 * (part % 2), 2), :, :, pl.ds(0, WIDTH)] = block_rows.reshape(2, 4, 32, WIDTH)
        tiny = dot(small[...].astype(BF16), norm_places()).T.astype(BF16)
        o_low[:, :, :, :, pl.ds(WIDTH, 128)] = tiny.reshape(2, 4, 4, 32, 128)
        core_o = mail.go(o_low.at[1 - me.c], o_core, mail.block(1), me.core_peer())

        keep["core_out"].wait_recv()

        def add_out(j, carry):
            gwo[j, me.c] = (gwo[j, me.c].astype(F32) + got_out[j].astype(F32)).astype(BF16)
            return carry

        lax.fori_loop(0, 8, add_out, 0)
        s_yo = mail.block(4)
        ys_out = [
            mail.go(gwo.at[2 * xx + 1 - me.y, me.c], y_out.at[xx], s_yo + xx, me.y_peer()) for xx in range(4)
        ]
        wait_all(fars)
        near_right = gwi.at[2 * right, me.c]
        near_right[...] = (near_right[...].astype(F32) + x_far[0].astype(F32)).astype(BF16)
        near_left = gwi.at[2 * left + 1, me.c]
        near_left[...] = (near_left[...].astype(F32) + x_far[1].astype(F32)).astype(BF16)
        ring_all = ring + [
            mail.go(near_right, x_near.at[0], s_ring + 2, me.x_peer(1)),
            mail.go(near_left, x_near.at[3], s_ring + 3, me.x_peer(3)),
        ]

        wait_all(das)
        grads = da[...].astype(F32)
        product = grads * own[...].astype(F32)
        sums = jnp.zeros((512, 128), F32)
        for h in range(3):
            at = (128, 192, 64)[h]
            inside = (lanes >= at) & (lanes < at + 64)
            total = jnp.sum(jnp.where(inside, product, 0.0), axis=1, keepdims=True)
            for half in range(2):
                factor = scale[:, pl.ds(3 * half + h, 1)]
                sums = jnp.where(iota((512, 128), 1) == 3 * half + h, total * factor, sums)
        drow[...] = sums.T
        accb[...] = jnp.zeros(accb.shape, F32)
        dq[...] = jnp.zeros(dq.shape, F32)
        s_ckv, s_ykv = mail.block(8), mail.block(4)

        def core_copy(rel, xx, y):
            part = rows(4 * xx + 2 * y + 1 - me.c, TOK)
            return mail.copy(dkv.at[part], core_kv.at[4 * rel + xx], s_ckv + 4 * rel + xx, me.core_peer())

        def attend(rel, y):
            half = 1 - rel
            for h in range(3):
                at = (128, 192, 64)[h]
                inside = (lanes >= at) & (lanes < at + 64)
                kept = jnp.where(inside, da[...].astype(F32), 0.0) * scale[:, pl.ds(3 * half + h, 1)]
                doexp[pl.ds(512 * h, 512), :] = kept.astype(BF16)

            def one(xx, carry):
                span = rows(2 * xx + y, 256)
                keys = kv[span, pl.ds(0, 256)]
                values = kv[span, pl.ds(128, 256)]
                for h in range(3):
                    cols = pl.ds(512 * h, 512)
                    back = dot_nt(values, doexp[cols, :])
                    part = p_ref[span, cols].astype(F32) * (back - drow[pl.ds(3 * half + h, 1), :])
                    ds[:, cols] = part.astype(BF16)
                    for k in range(2):
                        for t in range(4):
                            kind = jnp.clip(4 * xx + 2 * y + k - (4 * t + 2 * me.y + me.c), -2, 2) + 2
                            accb[h, kind] += part[128 * k : 128 * k + 128, 128 * t : 128 * t + 128]
                for h in range(3):
                    cols = pl.ds(512 * h, 512)
                    dq[pl.ds(64 * h, 64), :] += dot_tn(keys, ds[:, cols])[64 * h : 64 * h + 64]
                gk = dot(ds[...], qexp[...])
                gv = dot(p_ref[span, :], doexp[...])
                dkv[span, pl.ds(0, 128)] = gk[:, :128].astype(BF16)
                dkv[span, pl.ds(128, 128)] = (gk[:, 128:] + gv[:, :128]).astype(BF16)
                dkv[span, pl.ds(256, 128)] = gv[:, 128:].astype(BF16)
                core_copy(rel, xx, y).start()
                return carry

            lax.fori_loop(0, 4, one, 0)

        attend(0, 1 - me.y)

        def to_y(xx):
            return mail.copy(y_send.at[xx], y_kv.at[xx], s_ykv + xx, me.y_peer())

        def forward_y(xx, carry):
            core_copy(0, xx, 1 - me.y).wait_recv()
            part = dkv[rows(4 * xx + 2 * (1 - me.y) + me.c, TOK), :].astype(F32)
            y_send[xx] = (part + core_kv[xx].astype(F32)).astype(BF16)
            to_y(xx).start()
            return carry

        lax.fori_loop(0, 4, forward_y, 0)

        class Sum:
            def __init__(self, low, core, z_got, mid2, q_got, last, x_got, first):
                self.low, self.core, self.z_got = low, core, z_got
                self.mid2, self.q_got, self.last, self.x_got = mid2, q_got, last, x_got
                self.first = first

            def peer(self, axis, k):
                return me.z_peer(k) if axis == "z" else me.q_peer(k)

            def of(self, axis, k):
                return me.z_of(k) if axis == "z" else me.q_of(k)

            def begin(self):
                self.copies = [mail.go(self.low.at[1 - me.c], self.core, mail.block(1), me.core_peer())]

            def part(self, index):
                return self.low.at[me.c, :, index] if self.first == "q" else self.low.at[me.c, index]

            def stage_one(self):
                wait_all(self.copies)
                total = self.low[me.c].astype(F32) + self.core[...].astype(F32)
                self.low[me.c] = total.astype(BF16)
                base = mail.block(4)
                self.copies = [
                    mail.go(self.part(self.of(self.first, k)), self.z_got.at[k - 1], base + k, self.peer(self.first, k))
                    for k in near
                ]

            def stage_two(self):
                wait_all(self.copies)
                total = self.part(me.q if self.first == "q" else me.z)[...].astype(F32)
                for k in range(3):
                    total = total + self.z_got[k].astype(F32)
                self.mid2[...] = total.astype(BF16)
                base = mail.block(4)
                second = "z" if self.first == "q" else "q"
                self.copies = [
                    mail.go(self.mid2.at[self.of(second, k)], self.q_got.at[k - 1], base + k, self.peer(second, k))
                    for k in near
                ]

            def stage_three(self):
                wait_all(self.copies)
                total = self.mid2[me.z if self.first == "q" else me.q].astype(F32)
                for k in range(3):
                    total = total + self.q_got[k].astype(F32)
                self.last[...] = total
                base = mail.block(4)
                self.copies = [
                    mail.go(self.last.at[rows(me.x_of(k), 8)], self.x_got.at[me.x], base + k, me.x_peer(k)) for k in near
                ]
                self.x_got[me.x] = self.last[rows(me.x, 8), :]

            def finish(self):
                wait_all(self.copies)

        of_out = Sum(o_low, o_core, o_z, o_mid2, o_q, o_last, o_x, "z")
        of_out.copies = [core_o]
        of_q = Sum(q_low, q_core, q_z, q_mid2, q_q, q_last, q_x, "z")
        of_kv = Sum(k_low, k_core, k_z, k_mid2, k_q, k_last, k_x, "q")
        of_out.stage_one()

        attend(1, me.y)

        fin_q[...] = (dq[...] * SCALE).T.astype(BF16)
        s_xq, s_xkv = mail.block(4), mail.block(4)
        home = [mail.go(fin_q.at[rows(me.x_of(k), TOK)], home_q.at[me.x], s_xq + k, me.x_peer(k)) for k in near]
        home_q[me.x] = fin_q[mine, :]
        wait_all(ns)
        for part in range(4):
            span = pl.ds(256 * part, 256)
            block_rows = dot_tn(norm_all[:, span], fin_q[...]).astype(BF16)
            q_low[part // 2, pl.ds(2 * (part % 2), 2)] = block_rows.reshape(2, 4, 32, fin_q.shape[1])
        of_q.begin()
        for k in near + [0]:
            xx = me.x_of(k)
            core_copy(1, xx, me.y).wait_recv()
            to_y(xx).wait_recv()
            part = dkv[rows(4 * xx + 2 * me.y + me.c, TOK), :].astype(F32)
            part = (part + core_kv[4 + xx].astype(F32) + y_kv[xx].astype(F32)).astype(BF16)
            fin_kv[rows(xx, TOK), :] = part
            if k:
                home.append(mail.go(fin_kv.at[rows(xx, TOK)], home_kv.at[me.x], s_xkv + k, me.x_peer(k)))
            else:
                home_kv[me.x] = part
        for part in range(4):
            span = pl.ds(256 * part, 256)
            block_rows = dot_tn(norm_all[:, span], fin_kv[...]).astype(BF16)
            k_low[part // 2, pl.ds(2 * (part % 2), 2)] = block_rows.reshape(2, 4, 32, fin_kv.shape[1])
        of_kv.begin()
        of_q.stage_one()
        of_out.stage_two()

        of_kv.stage_one()
        before, center, after = bucket_tile(tile - 128), bucket_tile(tile), bucket_tile(tile + 128)

        def bucket_sum(b, carry):
            for h in range(3):
                near_sum = (
                    jnp.where(before == b, accb[h, 1], 0.0)
                    + jnp.where(center == b, accb[h, 2], 0.0)
                    + jnp.where(after == b, accb[h, 3], 0.0)
                )
                trow[h, pl.ds(b, 1), :] = jnp.sum(near_sum, axis=0, keepdims=True)
            return carry

        lax.fori_loop(0, BUCKETS, bucket_sum, 0)
        table = jnp.zeros((BUCKETS, 128), F32)
        for h in range(3):
            trow[h, pl.ds(BUCKETS // 2 - 1, 1), :] += jnp.sum(accb[h, 0], axis=0, keepdims=True)
            trow[h, pl.ds(BUCKETS - 1, 1), :] += jnp.sum(accb[h, 4], axis=0, keepdims=True)
            total = jnp.sum(trow[h], axis=1, keepdims=True)
            table = jnp.where(iota((BUCKETS, 128), 1) == 3 * me.x + h, total, table)
        tabs[0] = table
        t_core = mail.go(tabs.at[0], t_got.at[0], mail.block(1), me.core_peer())

        wait_all(ring_all)
        for j in range(2):
            total = gwi[2 * me.x + j, me.c].astype(F32) + x_near[j].astype(F32) + x_near[2 + j].astype(F32)
            gwi[2 * me.x + j, me.c] = total.astype(BF16)
        y_hop = mail.go(gwi.at[2 * me.x + 1 - me.y, me.c], y_in, mail.block(1), me.y_peer())
        wait_all(ys_out)
        for xx in range(4):
            y_out[xx] = (gwo[2 * xx + me.y, me.c].astype(F32) + y_out[xx].astype(F32)).astype(BF16)
        s_zf, s_zn = mail.block(2), mail.block(4)
        z_fars = [
            mail.go(y_out.at[far, pl.ds(0, 96)], z_far.at[0], s_zf, me.x_peer(1)),
            mail.go(y_out.at[far, pl.ds(96, 96)], z_far.at[1], s_zf + 1, me.x_peer(3)),
        ]
        z_ring = [
            mail.go(y_out.at[right, pl.ds(96, 96)], z_near.at[1], s_zn, me.x_peer(1)),
            mail.go(y_out.at[left, pl.ds(0, 96)], z_near.at[2], s_zn + 1, me.x_peer(3)),
        ]
        of_q.stage_two()
        of_out.stage_three()
        t_core.wait_recv()
        tabs[1] = tabs[0] + t_got[0]
        s_tz = mail.block(4)
        ts = [mail.go(tabs.at[1], t_got.at[k], s_tz + k, me.z_peer(k)) for k in near]
        of_kv.stage_two()

        wait_all(home)

        def piece(p, j):
            g, t = j // 3, j % 3
            if p == 0:
                return home_q[g, :, pl.ds(128 * (t // 2), 128)].astype(F32), t % 2
            if p == 1:
                return home_kv[g, :, pl.ds(128 * (t // 2), 128)].astype(F32), t % 2
            at, half = ((2, 0), (2, 1), (1, 1))[t]
            return home_kv[g, :, pl.ds(128 * at, 128)].astype(F32), half

        for p in range(3):
            for n in range(6):
                first, half_first = piece(p, 2 * n)
                second, half_second = piece(p, 2 * n + 1)
                dproj[p, :, pl.ds(128 * n, 128)] = pair(first, half_first, second, half_second).astype(BF16)
        gnorm = dot_nt(dproj[0], w_ref[0]) + dot_nt(dproj[1], w_ref[1]) + dot_nt(dproj[2], w_ref[2])
        inputs = inp_ref[...].astype(F32)
        root1 = lax.rsqrt(jnp.mean(inputs * inputs, axis=1, keepdims=True) + EPSILON)
        gain1 = gain1_ref[...].reshape(1, WIDTH)
        u = gain1 * gnorm
        mean = jnp.mean(u * inputs, axis=1, keepdims=True)
        gin_ref[...] = gmid[...] + root1 * u - inputs * (root1 * root1 * root1 * mean)

        of_q.stage_three()
        wait_all(ts)
        tabs[2] = tabs[1] + t_got[1] + t_got[2] + t_got[3]
        s_tq = mail.block(4)
        ts = [mail.go(tabs.at[2], t_got.at[3 + k], s_tq + k, me.q_peer(k)) for k in near]
        wait_all(z_fars)
        y_out[right, pl.ds(0, 96), :] = (
            y_out[right, pl.ds(0, 96), :].astype(F32) + z_far[0].astype(F32)
        ).astype(BF16)
        y_out[left, pl.ds(96, 96), :] = (
            y_out[left, pl.ds(96, 96), :].astype(F32) + z_far[1].astype(F32)
        ).astype(BF16)
        z_ring = z_ring + [
            mail.go(y_out.at[right, pl.ds(0, 96)], z_near.at[0], s_zn + 2, me.x_peer(1)),
            mail.go(y_out.at[left, pl.ds(96, 96)], z_near.at[3], s_zn + 3, me.x_peer(3)),
        ]
        of_kv.stage_three()
        wait_all(ts)
        tabs[3] = tabs[2] + t_got[4] + t_got[5] + t_got[6]
        s_tx = mail.block(4)
        ts = [mail.go(tabs.at[3], t_got.at[6 + k], s_tx + k, me.x_peer(k)) for k in near]

        row = iota((16, WIDTH), 0)
        pick = (iota((16, WIDTH), 1) == 6 * (8 * me.i + me.e) + row) & (row < 6)
        pick = pick.astype(F32).astype(BF16)
        picked = [dot(pick, w_ref[p])[:8] for p in range(3)]
        gain_col = jnp.sum(jnp.where(pick[:8].astype(F32) > 0, gain1, 0.0), axis=1, keepdims=True)

        of_out.finish()
        total = o_x[0] + o_x[1] + o_x[2] + o_x[3]
        gout_ref[...] = total
        y_hop.wait_recv()
        gwin_ref[...] = gwi[2 * me.x + me.y, me.c].astype(F32) + y_in[...].astype(F32)
        wait_all(z_ring)
        gwout_ref[pl.ds(0, 96), :] = (
            y_out[me.x, pl.ds(0, 96), :].astype(F32) + z_near[0].astype(F32) + z_near[2].astype(F32)
        )
        gwout_ref[pl.ds(96, 96), :] = (
            y_out[me.x, pl.ds(96, 96), :].astype(F32) + z_near[1].astype(F32) + z_near[3].astype(F32)
        )
        wait_all(ts)
        gtable_ref[...] = tabs[3] + t_got[7] + t_got[8] + t_got[9]
        of_q.finish()
        of_kv.finish()

        def found(p, j):
            g, t = j // 3, j % 3
            if p == 0:
                return q_x[g, :, pl.ds(128 * (t // 2), 128)], t % 2
            if p == 1:
                return k_x[g, :, pl.ds(128 * (t // 2), 128)], t % 2
            at, half = ((2, 0), (2, 1), (1, 1))[t]
            return k_x[g, :, pl.ds(128 * at, 128)], half

        with_gain = jnp.zeros((8, 1), F32)
        for p in range(3):
            for n in range(6):
                first, half_first = found(p, 2 * n)
                second, half_second = found(p, 2 * n + 1)
                cols = pl.ds(128 * n, 128)
                part = pair(first, half_first, second, half_second)
                gqkv_ref[p, :, cols] = part
                with_gain = with_gain + jnp.sum(
                    part * picked[p][:, 128 * n : 128 * n + 128], axis=1, keepdims=True
                )
        real = iota((8, 1), 0) < 6
        gain_ref[...] = jnp.where(real, with_gain / jnp.where(real, gain_col, 1.0), 0.0) * jnp.ones((8, 128), F32)
        for copy in mail.started:
            copy.wait_send()
        for rel, y in ((0, 1 - me.y), (1, me.y)):
            for xx in range(4):
                core_copy(rel, xx, y).wait_send()
        for xx in range(4):
            to_y(xx).wait_send()

    pl.run_scoped(
        rest,
        pltpu.VMEM((1536, 256), BF16),
        pltpu.VMEM((128, 512), F32),
        pltpu.VMEM((3, 5, 128, 128), F32),
        pltpu.VMEM((256, 1536), BF16),
        pltpu.VMEM((256, 512), F32),
        pltpu.VMEM((2048, 384), BF16),
        pltpu.VMEM((4, TOK, 384), BF16),
        pltpu.VMEM((512, 384), BF16),
        pltpu.VMEM((512, 256), BF16),
        pltpu.VMEM((3, TOK, WIDTH), BF16),
        pltpu.VMEM((2, 4, 4, 32, WIDTH + 128), BF16),
        pltpu.VMEM((2, 4, 4, 32, 256), BF16),
        pltpu.VMEM((2, 4, 4, 32, 384), BF16),
    )


def sum_buffers(width):
    return [
        pltpu.VMEM((4, 4, 32, width), BF16),
        pltpu.VMEM((3, 4, 32, width), BF16),
        pltpu.VMEM((4, 32, width), BF16),
        pltpu.VMEM((3, 32, width), BF16),
        pltpu.VMEM((32, width), F32),
        pltpu.VMEM((4, 8, width), F32),
    ]


def layer(*arrays):
    shape = jax.ShapeDtypeStruct
    vm = pltpu.VMEM
    return pl.pallas_call(
        layer_kernel,
        out_shape=(
            shape((TOK, WIDTH), BF16),
            shape((TOK, WIDTH), F32),
            shape((48, FF), F32),
            shape((192, WIDTH), F32),
            shape((3, 8, WIDTH), F32),
            shape((8, WIDTH + 128), F32),
            shape((8, 128), F32),
            shape((BUCKETS, 128), F32),
        ),
        in_specs=[VMEM] * 3 + [SMEM] + [VMEM] * 4 + [ANY] * 2 + [VMEM],
        out_specs=(VMEM,) * 8,
        scratch_shapes=[
            vm((512, 1024), BF16),
            vm((TOK, 1024), BF16),
            vm((512, 256), BF16),
            vm((2048, 384), BF16),
            vm((1536, 256), BF16),
            vm((2048, 1536), BF16),
            vm((512, 128), F32),
            vm((512, 256), BF16),
            vm((4, TOK, 256), BF16),
            vm((TOK, WIDTH), F32),
            vm((2 * TOK, 16 * CAP), BF16),
            vm((16 * CAP, WIDTH), BF16),
            vm((16 * CAP, WIDTH), BF16),
            vm((16 * CAP, WIDTH), BF16),
            vm((8, 2, 48, FF), BF16),
            vm((8, 2, 192, WIDTH), BF16),
            vm((TOK, WIDTH), F32),
            vm((TOK, WIDTH), BF16),
            vm((4, TOK, 256), BF16),
            vm((512, 256), BF16),
            vm((8, TOK, 384), BF16),
            vm((4, TOK, 384), BF16),
            vm((4, TOK, 256), BF16),
            vm((4, TOK, 384), BF16),
            vm((128, WIDTH), F32),
        ]
        + sum_buffers(WIDTH + 128)
        + sum_buffers(256)
        + sum_buffers(384)
        + [
            vm((3, BUCKETS, 128), F32),
            vm((4, BUCKETS, 128), F32),
            vm((10, BUCKETS, 128), F32),
            vm((8, 48, FF), BF16),
            vm((8, 192, WIDTH), BF16),
            vm((2, 48, FF), BF16),
            vm((4, 48, FF), BF16),
            vm((48, FF), BF16),
            vm((4, 192, WIDTH), BF16),
            vm((2, 96, WIDTH), BF16),
            vm((4, 96, WIDTH), BF16),
            pltpu.SemaphoreType.DMA((2,)),
            pltpu.SemaphoreType.DMA((SEMS,)),
            pltpu.SemaphoreType.DMA((SEMS,)),
        ],
        compiler_params=pltpu.CompilerParams(
            collective_id=0, has_side_effects=True, vmem_limit_bytes=VMEM_LIMIT
        ),
    )(*arrays)


def body(
    block_input, gain_one, qkv_weight, out_weight, rel_table, gain_two, router_weight, routes, w_in, w_out, cotangent
):
    y, gin, gwin, gwout, gqkv, gout, gain, table = layer(
        block_input[0], gain_one, qkv_weight, rel_table.T, out_weight, gain_two, router_weight.T,
        routes.reshape(1, TOK), w_in.reshape(8, 2, 48, FF), w_out.reshape(8, 2, 192, WIDTH), cotangent[0],
    )
    return (
        y[None],
        gin[None],
        gain[:6, 0],
        gqkv[:, :6],
        gout[:6, :WIDTH],
        table[:, :HEADS],
        gout[:6, WIDTH],
        gout[:6, WIDTH + 8 : WIDTH + 16],
        gwin[None],
        gwout[None],
    )


def solution(mesh):
    tokens = P("expert", "ctx", None)
    split = P(("ctx", "expert"))
    return jax.shard_map(
        body,
        mesh=mesh,
        in_specs=(
            tokens, P(), P(), P(), P(), P(), P(), tokens, P("expert", None, None), P("expert", None, None), tokens,
        ),
        out_specs=(
            tokens, tokens, split, P(None, ("ctx", "expert"), None), split, P(), split, split, tokens, tokens,
        ),
        check_vma=False,
    )
```

time: 1690 us -> 152 us (0.09)
  starting transfers between devices: 425 us -> 0 us
  blocking collectives: 416 us -> 0 us
  local copies, waits for them, and re-layouts: 291 us -> 14.2 us
  other arithmetic: 254 us -> 0 us
  matrix products: 182 us -> 0 us
  Pallas kernels: 0 us -> 137 us
  waiting for transfers between devices: 92.9 us -> 0 us
    unnamed x2 -> x0, blocking collectives: 416 us -> none
    ppermute x64 -> x0, starting transfers between devices: 306 us -> none  [from_behind(): return lax.ppermute(value, axis, pairs)]
    dot_general x114 -> x0, matrix products: 182 us -> none  [the longest x16 32.7 us: block_grads(): jnp.einsum('hqk,khd->qhd', grad_raw, key_heads, preferred_element_type=jn...]
    pallas_call x0 -> x1, Pallas kernels: none -> 137 us  [layer(): pl.pallas_call(layer_kernel, out_shape=(shape((TOK, WIDTH), BF16), shape(...]
    unnamed x33 -> x0, starting transfers between devices: 99.4 us -> none
    convert_element_type x69 -> x0, other arithmetic: 83.8 us -> none  [the longest x32 54.3 us: turn(): part.astype(own.dtype)]
    while x303 -> x0, local copies, waits for them, and re-layouts: 75.3 us -> none
    add x99 -> x0, other arithmetic: 73.6 us -> none  [the longest x16 30.4 us: step_keys(): local[0] + grad_query]
  transfers between devices with their start and end apart: 105 -> 0, of which waited for: 7 -> 0; matrix products, arithmetic and copies ran while one was open for 52% -> 0% of each run, Pallas kernels for 0% -> 0%
where the time goes in v2:
time: 152 us
  Pallas kernels  137 us (90%)
  local copies, waits for them, and re-layouts  14.2 us (9%)
    pallas_call x1, Pallas kernels, layer(): pl.pallas_call(layer_kernel, out_shape=(shape((TOK, WIDTH), BF16), shape(...  137 us
    unnamed x6, local copies, waits for them, and re-layouts  10.1 us

profile of v2, /device:TPU:1, one launch (start us, length us, event | category | flops | bytes accessed | tf_op | source)
XLA Modules:
  0.0 151.9 jit_solution(5071741088757051418)
XLA Ops:
  0.6 137.1 %shard_map.186 = (bf16[128,768]{1,0:T(8,128)(2,1)}, f32[128,768]{1,0:T(8,128)}, f32[48,3072]{1,0:T(8,128)}, f32[192,768]{1,0:T(8,128)}, f32[3,8,768]{2,1,0:T(8,1...) custom-call(bf16[128,768]{1,0:T(8,128)(2,1)} %bitcast.18, f32[768]{0:T(1024)} %gain1_ref.1, ...), custom_call_target="tpu_custom_call" | custom-call | tf_op jit(solution)/shard_map/pallas_call | solution.py:927
  137.7 1.4 slice_reduce_fusion
  139.1 1.3 slice.23
  140.4 1.3 slice.20
  141.8 1.4 copy.22
  143.2 1.6 %copy.28 = bf16[1,128,768]{2,1,0:T(8,128)(2,1)} copy(bf16[1,128,768]{2,1,0:T(8,128)(2,1)} %bitcast.20) | data formatting | bytes 393216
  144.8 1.8 %copy.29 = f32[1,128,768]{2,1,0:T(8,128)} copy(f32[1,128,768]{2,1,0:T(8,128)} %bitcast.17) | data formatting | bytes 786432
  146.5 1.5 %copy.30 = f32[3,6,768]{2,1,0:T(8,128)} copy(f32[3,6,768]{2,1,0:T(8,128)} %bitcast.21) | data formatting | bytes 110592
  148.1 1.9 %copy.31 = f32[1,48,3072]{2,1,0:T(8,128)} copy(f32[1,48,3072]{2,1,0:T(8,128)} %bitcast.16) | data formatting | bytes 1179648
  150.0 1.9 %copy.32 = f32[1,192,768]{2,1,0:T(8,128)} copy(f32[1,192,768]{2,1,0:T(8,128)} %bitcast.15) | data formatting | bytes 1179648

commit v3 on v2

--- a/solution.py
+++ b/solution.py
@@ -259,7 +259,7 @@
 
     tile = iota((128, 128), 0) - iota((128, 128), 1)
     lanes = iota((512, 256), 1)
-    def attention(s_ref, bias, m_ref, l_ref, acc, o_part, o_t, kv_send, q_send):
+    def attention(s_ref, bias, m_ref, l_ref, acc, o_part, o_t, kv_send, q_send, q_turned):
         for g in range(4):
             a = 3 * g
             kv_send[g, :, pl.ds(0, 128)] = join(1, a, 1, a + 1).astype(BF16)
@@ -292,30 +292,37 @@
             bias[h, 4] = jnp.full((128, 128), 1.0, F32) * table_ref[head, BUCKETS - 1]
         m_ref[...] = jnp.full(m_ref.shape, -jnp.inf, F32)
         l_ref[...] = jnp.zeros(l_ref.shape, F32)
+        for k in near:
+            kvs[k].wait_recv()
+            pass_on(k)
         wait_all(qs.values())
         queries = q_all[...].astype(F32) * SCALE
         for h in range(3):
             inside = (lanes >= 64 * h) & (lanes < 64 * h + 64)
-            qexp[pl.ds(512 * h, 512), :] = jnp.where(inside, queries, 0.0).astype(BF16)
-
-        def score(first, last, half, y, c):
-            def one(step, carry):
-                xx = me.x_of(-step)
-                b = 4 * xx + 2 * y + c
-                keys = kv[rows(b, TOK), pl.ds(0, 256)]
-                for h in range(3):
-                    s = dot_nt(keys, qexp[pl.ds(512 * h, 512), :])
-                    for t in range(4):
-                        kind = jnp.clip(b - (4 * t + 2 * me.y + me.c), -2, 2) + 2
-                        part = s[:, 128 * t : 128 * t + 128] + bias[h, kind]
-                        cols = pl.ds(128 * t, 128)
-                        s_ref[h, rows(2 * xx + c, TOK), cols] = part
-                        m_ref[half, h, :, cols] = jnp.maximum(
-                            m_ref[half, h, :, cols], jnp.max(part.reshape(16, 8, 128), axis=0)
-                        )
-                return carry
-
-            lax.fori_loop(first, last, one, 0)
+            part = jnp.where(inside, queries, 0.0)
+            qexp[pl.ds(512 * h, 512), :] = part.astype(BF16)
+            q_turned[:, pl.ds(512 * h, 512)] = part.T.astype(BF16)
+
+        def score(steps, half, y):
+            for h in range(3):
+                turned = q_turned[:, pl.ds(512 * h, 512)]
+
+                def one(step, carry):
+                    xx = me.x_of(-step)
+                    s = dot(kv[rows(2 * xx + y, 256), pl.ds(0, 256)], turned)
+                    for k in range(2):
+                        b = 4 * xx + 2 * y + k
+                        for t in range(4):
+                            kind = jnp.clip(b - (4 * t + 2 * me.y + me.c), -2, 2) + 2
+                            part = s[128 * k : 128 * k + 128, 128 * t : 128 * t + 128] + bias[h, kind]
+                            cols = pl.ds(128 * t, 128)
+                            s_ref[h, rows(2 * xx + k, TOK), cols] = part
+                            m_ref[half, h, :, cols] = jnp.maximum(
+                                m_ref[half, h, :, cols], jnp.max(part.reshape(16, 8, 128), axis=0)
+                            )
+                    return carry
+
+                lax.fori_loop(steps[0], steps[1], one, 0)
 
         def weigh(half, y):
             for h in range(3):
@@ -335,14 +342,11 @@
                 at = pl.ds((128, 192, 64)[h], 64)
                 o_part[half, at, :] = acc[at, :]
 
-        score(0, 1, 0, me.y, me.c)
+        cs[0].wait_recv()
+        score((0, 1), 0, me.y)
         for k in near:
-            kvs[k].wait_recv()
-            pass_on(k)
-        score(1, 4, 0, me.y, me.c)
-        for k in range(4):
             cs[k].wait_recv()
-        score(0, 4, 0, me.y, 1 - me.c)
+        score((1, 4), 0, me.y)
         fs = {}
         for k in (0, 1, 3, 2):
             ys[k].wait_recv()
@@ -353,9 +357,8 @@
 
             fs[k] = mail.go_later(to)
         weigh(0, me.y)
-        score(0, 4, 1, 1 - me.y, me.c)
         wait_all(fs.values())
-        score(0, 4, 1, 1 - me.y, 1 - me.c)
+        score((0, 4), 1, 1 - me.y)
         weigh(1, 1 - me.y)
 
         factors = jnp.zeros((128, 512), F32)
@@ -388,10 +391,10 @@
         pltpu.VMEM((256, 512), F32),
         pltpu.VMEM((4, TOK, 384), BF16),
         pltpu.VMEM((4, TOK, 256), BF16),
+        pltpu.VMEM((256, 1536), BF16),
     )
     s_o, s_n = mail.block(4), mail.block(4)
     os = [mail.go(own.at[rows(me.x_of(k), TOK)], att.at[me.x], s_o + k, me.x_peer(k)) for k in near]
-    ns = [mail.go(norm_own, norm_all.at[mine], s_n + k, me.x_peer(k)) for k in near]
     att[me.x] = own[mine, :]
 
     s_there, s_home = mail.block(8), mail.block(8)
@@ -405,6 +408,7 @@
         load_out = pltpu.make_async_copy(w_out_hbm, gwo, local.at[1])
         load_out.start()
         wait_all(os)
+        ns = [mail.go_later(lambda k=k: (norm_own, norm_all.at[mine], s_n + k, me.x_peer(k))) for k in near]
         mixed = inputs
         for g in range(4):
             mixed = mixed + dot(att[g, :, pl.ds(0, 128)], out_w_ref[pl.ds(192 * g + 64, 128), :])
@@ -477,6 +481,13 @@
         ]
         back_got[slots, :] = rows_out[slots, :]
 
+        def grads_out(j, carry):
+            gwo[j] = dot_tn(hidden[:, rows(j, 384)], gprod[...]).astype(BF16).reshape(2, 192, WIDTH)
+            return carry
+
+        lax.fori_loop(0, 8, grads_out, 0)
+        s_out = mail.block(1)
+        keep["core_out"] = mail.go_later(lambda: (gwo.at[:, 1 - me.c], got_out, s_out, me.core_peer()))
         def grads_in(j, carry):
             cols = rows(j, 256)
             gwi[:, :, :, cols] = dot_tn(arrived[...], ginner[:, cols]).astype(BF16).reshape(8, 2, 48, 256)
@@ -486,13 +497,7 @@
         s_in = mail.block(1)
         keep["core_in"] = mail.go_later(lambda: (gwi.at[:, 1 - me.c], got_in, s_in, me.core_peer()))
 
-        def grads_out(j, carry):
-            gwo[j] = dot_tn(hidden[:, rows(j, 384)], gprod[...]).astype(BF16).reshape(2, 192, WIDTH)
-            return carry
-
-        lax.fori_loop(0, 8, grads_out, 0)
-        s_out = mail.block(1)
-        keep["core_out"] = mail.go_later(lambda: (gwo.at[:, 1 - me.c], got_out, s_out, me.core_peer()))
+        keep["norms"] = ns
         return gate, chosen, router, root, normed_two
 
     gate, chosen, router, root, normed_two = pl.run_scoped(
@@ -505,6 +510,21 @@
         pltpu.VMEM((8 * CAP, WIDTH), BF16),
     )
 
+    right, left, far = me.x_of(1), me.x_of(3), me.x_of(2)
+    keep["core_out"].wait_recv()
+
+    def add_out(j, carry):
+        gwo[j, me.c] = (gwo[j, me.c].astype(F32) + got_out[j].astype(F32)).astype(BF16)
+        return carry
+
+    lax.fori_loop(0, 8, add_out, 0)
+    s_yo = mail.block(4)
+
+    def over_y(k, xx):
+        return mail.go(gwo.at[2 * xx + 1 - me.y, me.c], y_out.at[xx], s_yo + k, me.y_peer())
+
+    ys_out = [over_y(0, far), over_y(1, right)]
+
     keep["core_in"].wait_recv()
 
     def add_in(j, carry):
@@ -513,17 +533,10 @@
 
     lax.fori_loop(0, 8, add_in, 0)
     s_far, s_ring = mail.block(2), mail.block(4)
-    right, left = me.x_of(1), me.x_of(3)
-    far = me.x_of(2)
     fars = [
         mail.go(gwi.at[2 * far, me.c], x_far.at[0], s_far, me.x_peer(1)),
         mail.go(gwi.at[2 * far + 1, me.c], x_far.at[1], s_far + 1, me.x_peer(3)),
     ]
-    ring = [
-        mail.go(gwi.at[2 * right + 1, me.c], x_near.at[1], s_ring, me.x_peer(1)),
-        mail.go(gwi.at[2 * left, me.c], x_near.at[2], s_ring + 1, me.x_peer(3)),
-    ]
-
     wait_all(keep["home"])
     returned = dot(select[pl.ds(0, TOK), :], back_got[...])
     gnorm = dot(select[pl.ds(TOK, TOK), :], back_got[...])
@@ -550,6 +563,10 @@
     s_da = mail.block(4)
     das = [mail.go(da_send.at[me.x_of(k)], da.at[mine], s_da + k, me.x_peer(k)) for k in near]
     da[mine, :] = da_send[me.x]
+    ring = [
+        mail.go(gwi.at[2 * right + 1, me.c], x_near.at[1], s_ring, me.x_peer(1)),
+        mail.go(gwi.at[2 * left, me.c], x_near.at[2], s_ring + 1, me.x_peer(3)),
+    ]
 
     def rest(doexp, drow, accb, ds, dq, dkv, y_send, fin_kv, fin_q, dproj, o_low, q_low, k_low):
         att_wide = dot(att[0], att_places(0))
@@ -563,17 +580,6 @@
         o_low[:, :, :, :, pl.ds(WIDTH, 128)] = tiny.reshape(2, 4, 4, 32, 128)
         core_o = mail.go(o_low.at[1 - me.c], o_core, mail.block(1), me.core_peer())
 
-        keep["core_out"].wait_recv()
-
-        def add_out(j, carry):
-            gwo[j, me.c] = (gwo[j, me.c].astype(F32) + got_out[j].astype(F32)).astype(BF16)
-            return carry
-
-        lax.fori_loop(0, 8, add_out, 0)
-        s_yo = mail.block(4)
-        ys_out = [
-            mail.go(gwo.at[2 * xx + 1 - me.y, me.c], y_out.at[xx], s_yo + xx, me.y_peer()) for xx in range(4)
-        ]
         wait_all(fars)
         near_right = gwi.at[2 * right, me.c]
         near_right[...] = (near_right[...].astype(F32) + x_far[0].astype(F32)).astype(BF16)
@@ -651,6 +657,7 @@
             return carry
 
         lax.fori_loop(0, 4, forward_y, 0)
+        y_rest = [over_y(2, left), over_y(3, me.x)]
 
         class Sum:
             def __init__(self, low, core, z_got, mid2, q_got, last, x_got, first):
@@ -711,7 +718,7 @@
         of_out = Sum(o_low, o_core, o_z, o_mid2, o_q, o_last, o_x, "z")
         of_out.copies = [core_o]
         of_q = Sum(q_low, q_core, q_z, q_mid2, q_q, q_last, q_x, "z")
-        of_kv = Sum(k_low, k_core, k_z, k_mid2, k_q, k_last, k_x, "q")
+        of_kv = Sum(k_low, k_core, k_z, k_mid2, k_q, k_last, k_x, "z")
         of_out.stage_one()
 
         attend(1, me.y)
@@ -720,7 +727,7 @@
         s_xq, s_xkv = mail.block(4), mail.block(4)
         home = [mail.go(fin_q.at[rows(me.x_of(k), TOK)], home_q.at[me.x], s_xq + k, me.x_peer(k)) for k in near]
         home_q[me.x] = fin_q[mine, :]
-        wait_all(ns)
+        wait_all(keep["norms"])
         for part in range(4):
             span = pl.ds(256 * part, 256)
             block_rows = dot_tn(norm_all[:, span], fin_q[...]).astype(BF16)
@@ -773,7 +780,7 @@
             total = gwi[2 * me.x + j, me.c].astype(F32) + x_near[j].astype(F32) + x_near[2 + j].astype(F32)
             gwi[2 * me.x + j, me.c] = total.astype(BF16)
         y_hop = mail.go(gwi.at[2 * me.x + 1 - me.y, me.c], y_in, mail.block(1), me.y_peer())
-        wait_all(ys_out)
+        wait_all(ys_out + y_rest)
         for xx in range(4):
             y_out[xx] = (gwo[2 * xx + me.y, me.c].astype(F32) + y_out[xx].astype(F32)).astype(BF16)
         s_zf, s_zn = mail.block(2), mail.block(4)
@@ -990,22 +997,62 @@
     )(*arrays)
 
 
+def place_kernel(
+    y, gin, gwin, gwout, gqkv, gout, gain, table,
+    y_ref, gin_ref, gwin_ref, gwout_ref, gqkv_ref, gout_ref, gain1_ref, gain2_ref, router_ref, table_ref,
+):
+    y_ref[...] = y[...]
+    gin_ref[...] = gin[...]
+    gwin_ref[...] = gwin[...]
+    gwout_ref[...] = gwout[...]
+    gqkv_ref[...] = gqkv[:, :6, :]
+    gout_ref[...] = gout[:6, :WIDTH]
+    gain1_ref[...] = gain[...].T[:1, :6]
+    others = gout[:, WIDTH:].T
+    gain2_ref[...] = others[:1, :6]
+    router_ref[...] = others[8:16, :6]
+    table_ref[...] = table[...].T[:HEADS]
+
+
+def place(*arrays):
+    shape = jax.ShapeDtypeStruct
+    return pl.pallas_call(
+        place_kernel,
+        out_shape=(
+            shape((TOK, WIDTH), BF16),
+            shape((TOK, WIDTH), F32),
+            shape((48, FF), F32),
+            shape((192, WIDTH), F32),
+            shape((3, 6, WIDTH), F32),
+            shape((6, WIDTH), F32),
+            shape((1, 6), F32),
+            shape((1, 6), F32),
+            shape((8, 6), F32),
+            shape((HEADS, BUCKETS), F32),
+        ),
+        in_specs=[VMEM] * 8,
+        out_specs=(VMEM,) * 10,
+        compiler_params=pltpu.CompilerParams(vmem_limit_bytes=VMEM_LIMIT),
+    )(*arrays)
+
+
 def body(
     block_input, gain_one, qkv_weight, out_weight, rel_table, gain_two, router_weight, routes, w_in, w_out, cotangent
 ):
-    y, gin, gwin, gwout, gqkv, gout, gain, table = layer(
+    parts = layer(
         block_input[0], gain_one, qkv_weight, rel_table.T, out_weight, gain_two, router_weight.T,
         routes.reshape(1, TOK), w_in.reshape(8, 2, 48, FF), w_out.reshape(8, 2, 192, WIDTH), cotangent[0],
     )
+    y, gin, gwin, gwout, gqkv, gout, gain1, gain2, router, table = place(*parts)
     return (
         y[None],
         gin[None],
-        gain[:6, 0],
-        gqkv[:, :6],
-        gout[:6, :WIDTH],
-        table[:, :HEADS],
-        gout[:6, WIDTH],
-        gout[:6, WIDTH + 8 : WIDTH + 16],
+        gain1.reshape(6),
+        gqkv,
+        gout,
+        table.T,
+        gain2.reshape(6),
+        router.T,
         gwin[None],
         gwout[None],
     )

time: 152 us -> 131 us (0.86)
  local copies, waits for them, and re-layouts: 14.2 us -> 1.35 us
  Pallas kernels: 137 us -> 129 us
    pallas_call x1, Pallas kernels: 137 us -> 126 us  [layer(): pl.pallas_call(layer_kernel, out_shape=(shape((TOK, WIDTH), BF16), shape(...]
    unnamed x6 -> x1, local copies, waits for them, and re-layouts: 10.1 us -> 1.35 us
    slice x3 -> x0, local copies, waits for them, and re-layouts: 4.03 us -> none  [the longest x1 1.35 us: body(): gout[:6, WIDTH]]
    pallas_call x0 -> x1, Pallas kernels: none -> 2.72 us  [place(): pl.pallas_call(place_kernel, out_shape=(shape((TOK, WIDTH), BF16), shape(...]
where the time goes in v3:
time: 131 us
  Pallas kernels  129 us (98%)
  local copies, waits for them, and re-layouts  1.35 us (1%)
    pallas_call x1, Pallas kernels, layer(): pl.pallas_call(layer_kernel, out_shape=(shape((TOK, WIDTH), BF16), shape(...  126 us
    pallas_call x1, Pallas kernels, place(): pl.pallas_call(place_kernel, out_shape=(shape((TOK, WIDTH), BF16), shape(...  2.72 us

profile of v3, /device:TPU:1, one launch (start us, length us, event | category | flops | bytes accessed | tf_op | source)
XLA Modules:
  0.0 131.1 jit_solution(10526242084123883217)
XLA Ops:
  0.6 126.3 %shard_map.186 = (bf16[128,768]{1,0:T(8,128)(2,1)}, f32[128,768]{1,0:T(8,128)}, f32[48,3072]{1,0:T(8,128)}, f32[192,768]{1,0:T(8,128)}, f32[3,8,768]{2,1,0:T(8,1...) custom-call(bf16[128,768]{1,0:T(8,128)(2,1)} %bitcast.17, f32[768]{0:T(1024)} %gain1_ref.1, ...), custom_call_target="tpu_custom_call" | custom-call | tf_op jit(solution)/shard_map/pallas_call | solution.py:934
  127.0 2.7 %shard_map.187 = (bf16[128,768]{1,0:T(8,128)(2,1)}, f32[128,768]{1,0:T(8,128)}, f32[48,3072]{1,0:T(8,128)}, f32[192,768]{1,0:T(8,128)}, f32[3,6,768]{2,1,0:T(8,1...) custom-call(bf16[128,768]{1,0:T(8,128)(2,1)} %get-tuple-element.28.y, ...), custom_call_target="tpu_custom_call" | custom-call | tf_op jit(solution)/shard_map/pallas_call | solution.py:1019
  129.7 1.4 %copy.21 = f32[6,8]{1,0:T(8,128)} copy(f32[6,8]{0,1:T(8,128)} %bitcast.21) | data formatting | bytes 384

commit v4 on v3

--- a/solution.py
+++ b/solution.py
@@ -322,7 +322,7 @@
                             )
                     return carry
 
-                lax.fori_loop(steps[0], steps[1], one, 0)
+                lax.fori_loop(steps[0], steps[1], one, 0, unroll=True)
 
         def weigh(half, y):
             for h in range(3):
@@ -338,7 +338,7 @@
                     acc[...] += dot_tn(kv[span, pl.ds(128, 256)], low)
                     return carry
 
-                lax.fori_loop(0, 4, one, 0)
+                lax.fori_loop(0, 4, one, 0, unroll=True)
                 at = pl.ds((128, 192, 64)[h], 64)
                 o_part[half, at, :] = acc[at, :]
 
@@ -460,15 +460,15 @@
                 t = jnp.tanh(slope * inner * (1.0 + 0.044715 * square))
                 half = 0.5 * (1.0 + t)
                 hidden[:, part] = (inner * half).astype(BF16)
-                w_out = gwo[pl.ds(2 * j, 2)].reshape(chunk, WIDTH)[256 * k : 256 * k + 256]
+                w_out = gwo[j].reshape(chunk, WIDTH)[256 * k : 256 * k + 256]
                 back = dot_nt(gprod[...], w_out)
                 lean = half + 0.5 * inner * (1.0 - t * t) * slope * (1.0 + 3 * 0.044715 * square)
                 ginner[:, part] = (lean * back).astype(BF16)
-            made[...] += dot(hidden[:, cols], gwo[pl.ds(2 * j, 2)].reshape(chunk, WIDTH))
+            made[...] += dot(hidden[:, cols], gwo[j].reshape(chunk, WIDTH))
             garr[...] += dot_nt(ginner[:, cols], gwi[:, :, :, cols].reshape(WIDTH, chunk))
             return carry
 
-        lax.fori_loop(0, FF // chunk, through, 0)
+        lax.fori_loop(0, FF // chunk, through, 0, unroll=2)
         back = jnp.concatenate([made[...].reshape(8, CAP, WIDTH), garr[...].reshape(8, CAP, WIDTH)], axis=1)
         for copy in there:
             mail.sent(copy)
@@ -481,21 +481,33 @@
         ]
         back_got[slots, :] = rows_out[slots, :]
 
-        def grads_out(j, carry):
-            gwo[j] = dot_tn(hidden[:, rows(j, 384)], gprod[...]).astype(BF16).reshape(2, 192, WIDTH)
-            return carry
-
-        lax.fori_loop(0, 8, grads_out, 0)
-        s_out = mail.block(1)
-        keep["core_out"] = mail.go_later(lambda: (gwo.at[:, 1 - me.c], got_out, s_out, me.core_peer()))
+        arrived_t = arrived[...].T
+
         def grads_in(j, carry):
             cols = rows(j, 256)
-            gwi[:, :, :, cols] = dot_tn(arrived[...], ginner[:, cols]).astype(BF16).reshape(8, 2, 48, 256)
+            gwi[:, :, :, cols] = dot(arrived_t, ginner[:, cols]).astype(BF16).reshape(8, 2, 48, 256)
             return carry
 
-        lax.fori_loop(0, FF // 256, grads_in, 0)
+        lax.fori_loop(0, FF // 256, grads_in, 0, unroll=4)
         s_in = mail.block(1)
         keep["core_in"] = mail.go_later(lambda: (gwi.at[:, 1 - me.c], got_in, s_in, me.core_peer()))
+
+        def grads_out(y):
+            def one(xx, carry):
+                part = dot_tn(hidden[:, rows(2 * xx + y, 384)], gprod[...])
+                gwo[xx, y] = part.astype(BF16).reshape(2, 192, WIDTH)
+                return carry
+
+            lax.fori_loop(0, 4, one, 0, unroll=2)
+
+        s_out = mail.block(2)
+        for rel in range(2):
+            grads_out(me.y if rel else 1 - me.y)
+            keep["core_out", rel] = mail.go_later(
+                lambda rel=rel: (
+                    gwo.at[:, me.y if rel else 1 - me.y, 1 - me.c], got_out.at[rel], s_out + rel, me.core_peer()
+                )
+            )
 
         keep["norms"] = ns
         return gate, chosen, router, root, normed_two
@@ -511,20 +523,6 @@
     )
 
     right, left, far = me.x_of(1), me.x_of(3), me.x_of(2)
-    keep["core_out"].wait_recv()
-
-    def add_out(j, carry):
-        gwo[j, me.c] = (gwo[j, me.c].astype(F32) + got_out[j].astype(F32)).astype(BF16)
-        return carry
-
-    lax.fori_loop(0, 8, add_out, 0)
-    s_yo = mail.block(4)
-
-    def over_y(k, xx):
-        return mail.go(gwo.at[2 * xx + 1 - me.y, me.c], y_out.at[xx], s_yo + k, me.y_peer())
-
-    ys_out = [over_y(0, far), over_y(1, right)]
-
     keep["core_in"].wait_recv()
 
     def add_in(j, carry):
@@ -538,6 +536,20 @@
         mail.go(gwi.at[2 * far + 1, me.c], x_far.at[1], s_far + 1, me.x_peer(3)),
     ]
     wait_all(keep["home"])
+    keep["core_out", 0].wait_recv()
+
+    def add_out(xx, carry):
+        gwo[xx, 1 - me.y, me.c] = (gwo[xx, 1 - me.y, me.c].astype(F32) + got_out[0, xx].astype(F32)).astype(BF16)
+        return carry
+
+    lax.fori_loop(0, 4, add_out, 0)
+    s_yo = mail.block(4)
+
+    def over_y(k, xx):
+        return mail.go(gwo.at[xx, 1 - me.y, me.c], y_out.at[xx], s_yo + k, me.y_peer())
+
+
+    ys_out = [over_y(0, far), over_y(1, right)]
     returned = dot(select[pl.ds(0, TOK), :], back_got[...])
     gnorm = dot(select[pl.ds(TOK, TOK), :], back_got[...])
     mid = middle[...]
@@ -642,7 +654,7 @@
                 core_copy(rel, xx, y).start()
                 return carry
 
-            lax.fori_loop(0, 4, one, 0)
+            lax.fori_loop(0, 4, one, 0, unroll=2)
 
         attend(0, 1 - me.y)
 
@@ -727,6 +739,21 @@
         s_xq, s_xkv = mail.block(4), mail.block(4)
         home = [mail.go(fin_q.at[rows(me.x_of(k), TOK)], home_q.at[me.x], s_xq + k, me.x_peer(k)) for k in near]
         home_q[me.x] = fin_q[mine, :]
+
+        def over_x(xx):
+            total = gwo[xx, me.y, me.c].astype(F32) + got_out[1, xx].astype(F32) + y_out[xx].astype(F32)
+            y_out[xx] = total.astype(BF16)
+
+        keep["core_out", 1].wait_recv()
+        wait_all(ys_out)
+        over_x(far)
+        over_x(right)
+        s_zf, s_zn = mail.block(2), mail.block(4)
+        z_fars = [
+            mail.go(y_out.at[far, pl.ds(0, 96)], z_far.at[0], s_zf, me.x_peer(1)),
+            mail.go(y_out.at[far, pl.ds(96, 96)], z_far.at[1], s_zf + 1, me.x_peer(3)),
+        ]
+        z_ring = [mail.go(y_out.at[right, pl.ds(96, 96)], z_near.at[1], s_zn, me.x_peer(1))]
         wait_all(keep["norms"])
         for part in range(4):
             span = pl.ds(256 * part, 256)
@@ -765,7 +792,7 @@
                 trow[h, pl.ds(b, 1), :] = jnp.sum(near_sum, axis=0, keepdims=True)
             return carry
 
-        lax.fori_loop(0, BUCKETS, bucket_sum, 0)
+        lax.fori_loop(0, BUCKETS, bucket_sum, 0, unroll=4)
         table = jnp.zeros((BUCKETS, 128), F32)
         for h in range(3):
             trow[h, pl.ds(BUCKETS // 2 - 1, 1), :] += jnp.sum(accb[h, 0], axis=0, keepdims=True)
@@ -780,18 +807,10 @@
             total = gwi[2 * me.x + j, me.c].astype(F32) + x_near[j].astype(F32) + x_near[2 + j].astype(F32)
             gwi[2 * me.x + j, me.c] = total.astype(BF16)
         y_hop = mail.go(gwi.at[2 * me.x + 1 - me.y, me.c], y_in, mail.block(1), me.y_peer())
-        wait_all(ys_out + y_rest)
-        for xx in range(4):
-            y_out[xx] = (gwo[2 * xx + me.y, me.c].astype(F32) + y_out[xx].astype(F32)).astype(BF16)
-        s_zf, s_zn = mail.block(2), mail.block(4)
-        z_fars = [
-            mail.go(y_out.at[far, pl.ds(0, 96)], z_far.at[0], s_zf, me.x_peer(1)),
-            mail.go(y_out.at[far, pl.ds(96, 96)], z_far.at[1], s_zf + 1, me.x_peer(3)),
-        ]
-        z_ring = [
-            mail.go(y_out.at[right, pl.ds(96, 96)], z_near.at[1], s_zn, me.x_peer(1)),
-            mail.go(y_out.at[left, pl.ds(0, 96)], z_near.at[2], s_zn + 1, me.x_peer(3)),
-        ]
+        wait_all(y_rest)
+        over_x(left)
+        over_x(me.x)
+        z_ring.append(mail.go(y_out.at[left, pl.ds(0, 96)], z_near.at[2], s_zn + 1, me.x_peer(3)))
         of_q.stage_two()
         of_out.stage_three()
         t_core.wait_recv()
@@ -961,7 +980,7 @@
             vm((16 * CAP, WIDTH), BF16),
             vm((16 * CAP, WIDTH), BF16),
             vm((8, 2, 48, FF), BF16),
-            vm((8, 2, 192, WIDTH), BF16),
+            vm((4, 2, 2, 192, WIDTH), BF16),
             vm((TOK, WIDTH), F32),
             vm((TOK, WIDTH), BF16),
             vm((4, TOK, 256), BF16),
@@ -980,7 +999,7 @@
             vm((4, BUCKETS, 128), F32),
             vm((10, BUCKETS, 128), F32),
             vm((8, 48, FF), BF16),
-            vm((8, 192, WIDTH), BF16),
+            vm((2, 4, 192, WIDTH), BF16),
             vm((2, 48, FF), BF16),
             vm((4, 48, FF), BF16),
             vm((48, FF), BF16),
@@ -1010,7 +1029,7 @@
     gain1_ref[...] = gain[...].T[:1, :6]
     others = gout[:, WIDTH:].T
     gain2_ref[...] = others[:1, :6]
-    router_ref[...] = others[8:16, :6]
+    router_ref[...] = gout[:6, WIDTH + 8 : WIDTH + 16]
     table_ref[...] = table[...].T[:HEADS]
 
 
@@ -1027,7 +1046,7 @@
             shape((6, WIDTH), F32),
             shape((1, 6), F32),
             shape((1, 6), F32),
-            shape((8, 6), F32),
+            shape((6, 8), F32),
             shape((HEADS, BUCKETS), F32),
         ),
         in_specs=[VMEM] * 8,
@@ -1041,7 +1060,7 @@
 ):
     parts = layer(
         block_input[0], gain_one, qkv_weight, rel_table.T, out_weight, gain_two, router_weight.T,
-        routes.reshape(1, TOK), w_in.reshape(8, 2, 48, FF), w_out.reshape(8, 2, 192, WIDTH), cotangent[0],
+        routes.reshape(1, TOK), w_in.reshape(8, 2, 48, FF), w_out.reshape(4, 2, 2, 192, WIDTH), cotangent[0],
     )
     y, gin, gwin, gwout, gqkv, gout, gain1, gain2, router, table = place(*parts)
     return (
@@ -1052,7 +1071,7 @@
         gout,
         table.T,
         gain2.reshape(6),
-        router.T,
+        router,
         gwin[None],
         gwout[None],
     )

time: 131 us -> 122 us (0.931)
  Pallas kernels: 129 us -> 121 us
  local copies, waits for them, and re-layouts: 1.35 us -> 0 us
    pallas_call x1, Pallas kernels: 126 us -> 118 us  [layer(): pl.pallas_call(layer_kernel, out_shape=(shape((TOK, WIDTH), BF16), shape(...]
    unnamed x1 -> x0, local copies, waits for them, and re-layouts: 1.35 us -> none
where the time goes in v4:
time: 122 us
  Pallas kernels  121 us (99%)
    pallas_call x1, Pallas kernels, layer(): pl.pallas_call(layer_kernel, out_shape=(shape((TOK, WIDTH), BF16), shape(...  118 us
    pallas_call x1, Pallas kernels, place(): pl.pallas_call(place_kernel, out_shape=(shape((TOK, WIDTH), BF16), shape(...  2.72 us

profile of v4, /device:TPU:1, one launch (start us, length us, event | category | flops | bytes accessed | tf_op | source)
XLA Modules:
  0.0 121.9 jit_solution(11630385651140784631)
XLA Ops:
  0.6 118.3 %shard_map.186 = (bf16[128,768]{1,0:T(8,128)(2,1)}, f32[128,768]{1,0:T(8,128)}, f32[48,3072]{1,0:T(8,128)}, f32[192,768]{1,0:T(8,128)}, f32[3,8,768]{2,1,0:T(8,1...) custom-call(bf16[128,768]{1,0:T(8,128)(2,1)} %bitcast.16, f32[768]{0:T(1024)} %gain1_ref.1, ...), custom_call_target="tpu_custom_call" | custom-call | tf_op jit(solution)/shard_map/pallas_call | solution.py:953
  119.0 2.7 %shard_map.187 = (bf16[128,768]{1,0:T(8,128)(2,1)}, f32[128,768]{1,0:T(8,128)}, f32[48,3072]{1,0:T(8,128)}, f32[192,768]{1,0:T(8,128)}, f32[3,6,768]{2,1,0:T(8,1...) custom-call(bf16[128,768]{1,0:T(8,128)(2,1)} %get-tuple-element.28.y, ...), custom_call_target="tpu_custom_call" | custom-call | tf_op jit(solution)/shard_map/pallas_call | solution.py:1038

commit v5 on v4

--- a/solution.py
+++ b/solution.py
@@ -468,7 +468,7 @@
             garr[...] += dot_nt(ginner[:, cols], gwi[:, :, :, cols].reshape(WIDTH, chunk))
             return carry
 
-        lax.fori_loop(0, FF // chunk, through, 0, unroll=2)
+        lax.fori_loop(0, FF // chunk, through, 0, unroll=True)
         back = jnp.concatenate([made[...].reshape(8, CAP, WIDTH), garr[...].reshape(8, CAP, WIDTH)], axis=1)
         for copy in there:
             mail.sent(copy)
@@ -529,7 +529,7 @@
         gwi[j, me.c] = (gwi[j, me.c].astype(F32) + got_in[j].astype(F32)).astype(BF16)
         return carry
 
-    lax.fori_loop(0, 8, add_in, 0)
+    lax.fori_loop(0, 8, add_in, 0, unroll=2)
     s_far, s_ring = mail.block(2), mail.block(4)
     fars = [
         mail.go(gwi.at[2 * far, me.c], x_far.at[0], s_far, me.x_peer(1)),
@@ -542,7 +542,7 @@
         gwo[xx, 1 - me.y, me.c] = (gwo[xx, 1 - me.y, me.c].astype(F32) + got_out[0, xx].astype(F32)).astype(BF16)
         return carry
 
-    lax.fori_loop(0, 4, add_out, 0)
+    lax.fori_loop(0, 4, add_out, 0, unroll=2)
     s_yo = mail.block(4)
 
     def over_y(k, xx):
@@ -654,7 +654,7 @@
                 core_copy(rel, xx, y).start()
                 return carry
 
-            lax.fori_loop(0, 4, one, 0, unroll=2)
+            lax.fori_loop(0, 4, one, 0, unroll=True)
 
         attend(0, 1 - me.y)
 

time: 122 us -> 121 us (level)
  no operation moved by 1% of the time
where the time goes in v5:
time: 121 us
  Pallas kernels  120 us (99%)
    pallas_call x1, Pallas kernels, layer(): pl.pallas_call(layer_kernel, out_shape=(shape((TOK, WIDTH), BF16), shape(...  117 us
    pallas_call x1, Pallas kernels, place(): pl.pallas_call(place_kernel, out_shape=(shape((TOK, WIDTH), BF16), shape(...  2.72 us

profile of v5, /device:TPU:1, one launch (start us, length us, event | category | flops | bytes accessed | tf_op | source)
XLA Modules:
  0.0 120.8 jit_solution(14729516948874345673)
XLA Ops:
  0.6 117.2 %shard_map.186 = (bf16[128,768]{1,0:T(8,128)(2,1)}, f32[128,768]{1,0:T(8,128)}, f32[48,3072]{1,0:T(8,128)}, f32[192,768]{1,0:T(8,128)}, f32[3,8,768]{2,1,0:T(8,1...) custom-call(bf16[128,768]{1,0:T(8,128)(2,1)} %bitcast.16, f32[768]{0:T(1024)} %gain1_ref.1, ...), custom_call_target="tpu_custom_call" | custom-call | tf_op jit(solution)/shard_map/pallas_call | solution.py:953
  117.9 2.7 %shard_map.187 = (bf16[128,768]{1,0:T(8,128)(2,1)}, f32[128,768]{1,0:T(8,128)}, f32[48,3072]{1,0:T(8,128)}, f32[192,768]{1,0:T(8,128)}, f32[3,6,768]{2,1,0:T(8,1...) custom-call(bf16[128,768]{1,0:T(8,128)(2,1)} %get-tuple-element.28.y, ...), custom_call_target="tpu_custom_call" | custom-call | tf_op jit(solution)/shard_map/pallas_call | solution.py:1038
